TPU v7x, 32 devices: a whole 2x2x4 slice. The times are simulated.
32 devices in a mesh: groups: 2 (over x), lon: 16 (over z, y, core).
Axes of the slice: x: 2, y: 2, z: 4, core: 2. Of those that a mesh axis runs over, the one named last changes fastest.
Arguments:
- atm_in: bfloat16 [256, 48, 640], P(('groups', 'lon')), parts along dimension 0, may hold values from -6 to 6
- ocean_in: bfloat16 [512, 95, 128], P(('groups', 'lon')), parts along dimension 0, may hold values from -6 to 6
- lift_weight: bfloat16 [48, 256], replicated, may hold values from -0.875 to 0.875
- conv_weight: bfloat16 [3, 3, 256, 256], replicated, may hold values from -0.125 to 0.125
- flux_weight: bfloat16 [256, 16], replicated, may hold values from -0.375 to 0.375
- ocean_weight: bfloat16 [95, 256], replicated, may hold values from -0.625 to 0.625
- couple_weight: bfloat16 [16, 256], replicated, may hold values from -3 to 3
- mix_weight: bfloat16 [256, 256], replicated, may hold values from -0.375 to 0.375
- regrid_weight: bfloat16 [256, 4, 128, 128], P('lon'), may hold values from 0 to 1, as said below
- pair_tile: int32 [256, 3], P('lon'), may hold values from 0 to 39, as said below
- ocean_mask: int32 [256], P('lon'), may hold values from 0 to 1, as said below
Outputs:
- atm_hidden: bfloat16 [256, 256, 640], P(('groups', 'lon')), parts along dimension 0
- ocean_hidden: bfloat16 [512, 256, 128], P(('groups', 'lon')), parts along dimension 0
There are 2 independent parts, one for each index of `groups`. A program takes and returns all parts, laid end to end along the dimension named above; an argument that names none is the same for every part. Nothing has to cross between parts.
Inputs may be any that keep to these rules, and one draw needn't show every extreme that they name: `regrid_weight`: block p = 3 is zero except for the northernmost 2 tiles of each strip (local index 14 and above); blocks 0 to 2 are positive. `pair_tile`: within one of the band of the ocean tile's latitude; column 1 is the band itself. `ocean_mask`: each device's 16 tiles hold between 2 and 8 ones, its northernmost 2 tiles always among them; some device has exactly 8.
All inputs are finite; a program needn't handle non-finite values.
Results may differ from a plain program's by a relative error of at most 0.0053.
Values may be sent and summed in bfloat16 or wider, within the bound.
A program may use at most 128 MiB of HBM per device.

v0:
```python
import jax
import jax.numpy as jnp
from jax import lax
from jax.sharding import PartitionSpec as P

TLAT = 16


def with_halo(block, sides, width):
    for axis, dim in sides:
        count = lax.axis_size(axis)
        forward = [(i, i + 1) for i in range(count - 1)]
        forward.append((count - 1, 0))
        backward = [(target, source) for source, target in forward]
        low = lax.ppermute(
            lax.slice_in_dim(block, block.shape[dim] - width, None, axis=dim), axis, forward
        )
        high = lax.ppermute(lax.slice_in_dim(block, 0, width, axis=dim), axis, backward)
        block = jnp.concatenate([low, block, high], axis=dim)
    return block


def partner(block, axis, bit):
    count = lax.axis_size(axis)
    route = []
    for low in range(count):
        high = low | 1 << bit
        if high != low and high < count:
            route += [(low, high), (high, low)]
    return lax.ppermute(block, axis, route)


def encode_ocean(states, blocks, got, ocean_weight, couple_weight, mix_weight):
    numer = jnp.einsum("spfa,spoa->sfo", got, blocks, preferred_element_type=jnp.float32)
    denom = jnp.sum(blocks, axis=(1, 3), dtype=jnp.float32)
    regrid = (numer / denom[:, None, :]).astype(jnp.bfloat16)
    base = jnp.einsum("sco,ch->sho", states, ocean_weight, preferred_element_type=jnp.float32)
    base = (
        base + jnp.einsum("sfo,fh->sho", regrid, couple_weight, preferred_element_type=jnp.float32)
    ).astype(jnp.bfloat16)
    mixed = jnp.einsum("sho,hk->sko", base, mix_weight, preferred_element_type=jnp.float32)
    return (base.astype(jnp.float32) + jax.nn.gelu(mixed)).astype(jnp.bfloat16)


def per_device(
    atm_in,
    ocean_in,
    lift_weight,
    conv_weight,
    flux_weight,
    ocean_weight,
    couple_weight,
    mix_weight,
    regrid_weight,
    pair_tile,
    ocean_mask,
):
    columns = atm_in.shape[0]
    lat_rows = atm_in.shape[2]
    hidden_width = lift_weight.shape[1]
    lifted = jnp.einsum(
        "xcy,co->xoy", atm_in, lift_weight, preferred_element_type=jnp.float32
    ).astype(jnp.bfloat16)
    padded = with_halo(lifted, (("lon", 0),), 1)
    padded = jnp.pad(padded, ((0, 0), (0, 0), (1, 1)))
    conv = jnp.zeros((columns, hidden_width, lat_rows), jnp.float32)
    for shift_x in range(3):
        for shift_y in range(3):
            conv = conv + jnp.einsum(
                "xcy,co->xoy",
                padded[shift_x : shift_x + columns, :, shift_y : shift_y + lat_rows],
                conv_weight[shift_x, shift_y],
                preferred_element_type=jnp.float32,
            )
    atm_hidden = (lifted.astype(jnp.float32) + jax.nn.gelu(conv)).astype(jnp.bfloat16)
    flux = jnp.einsum(
        "xhy,hf->xfy", atm_hidden, flux_weight, preferred_element_type=jnp.float32
    ).astype(jnp.bfloat16)
    flux_count = flux.shape[1]
    tiles_lat = lat_rows // TLAT
    tiles = (
        flux.reshape(columns, flux_count, tiles_lat, TLAT)
        .transpose(2, 1, 0, 3)
        .reshape(tiles_lat, flux_count, columns * TLAT)
    )
    near = with_halo(tiles[None], (("lon", 0),), 1)
    near = near.reshape((3 * tiles_lat,) + tiles.shape[1:])
    northern = tiles[tiles_lat - 1]
    strips = lax.axis_size("lon")
    mirrored = northern
    for bit in range(strips.bit_length() - 1):
        mirrored = partner(mirrored, "lon", bit)
    table = jnp.concatenate([near, mirrored[None]], 0)
    local_tiles = ocean_in.shape[0]
    index = jnp.concatenate(
        [
            pair_tile + jnp.arange(3, dtype=jnp.int32)[None, :] * tiles_lat,
            jnp.full((local_tiles, 1), 3 * tiles_lat, jnp.int32),
        ],
        1,
    )
    got = jnp.take(table, index, axis=0)
    result = encode_ocean(ocean_in, regrid_weight, got, ocean_weight, couple_weight, mix_weight)
    ocean_hidden = jnp.where(ocean_mask[:, None, None] == 1, result, jnp.zeros_like(result))
    return (atm_hidden, ocean_hidden)


def solution(mesh):
    in_specs = (
        P(("groups", "lon"), None, None),
        P(("groups", "lon"), None, None),
        P(),
        P(),
        P(),
        P(),
        P(),
        P(),
        P("lon", None, None, None),
        P("lon", None),
        P("lon"),
    )
    out_specs = (P(("groups", "lon"), None, None), P(("groups", "lon"), None, None))
    return jax.shard_map(
        per_device, mesh=mesh, in_specs=in_specs, out_specs=out_specs, check_vma=False
    )
```

profile of v0, /device:TPU:0, one launch (start us, length us, event | category | flops | bytes accessed | tf_op | source)
XLA Modules:
  0.0 97.4 jit_solution(10864364514326306454)
XLA Ops:
  1.7 1.6 %convert_bitcast_fusion = bf16[8,256,640]{2,1,0:T(8,128)(2,1)S(1)} fusion(bf16[8,48,640]{2,1,0:T(8,128)(2,1)S(1)} %copy-done, bf16[48,256]{1,0:T(8,128)(2,1)} %param.13), kind=kOutput, calls=%fused_computation.41 | convolution fusion | flops 127139840 | bytes 3137536 | tf_op jit(solution)/shard_map/xcy,co->xoy/dot_general | solution.py:61
  3.8 5.1 %collective-permute-start.1 = (bf16[1,256,640]{2,1,0:T(8,128)(2,1)S(1)}, bf16[1,256,640]{2,1,0:T(8,128)(2,1)S(1)}, u32[]{:S(2)}, u32[]{:S(2)}) collective-permute-start(bf16[1,256,640]{2,1,0:T(8,128)(2,1)S(1)} %get-tuple-element.3), channel_id=1, source_target_pairs={{1,0},{2,1},{3,2},{4,3},{5,4},{6,5},{7,6},{8,7},{9,8},{10,9},{11,1... | collective-permute-start | bytes 983048 | tf_op jit(solution)/shard_map/ppermute | solution.py:18
  8.9 3.2 %fusion.61 = f32[8,640,256]{1,2,0:T(8,128)} fusion(bf16[8,256,640]{2,1,0:T(8,128)(2,1)S(1)} %convert_bitcast_fusion, bf16[3,3,256,256]{3,2,1,0:T(8,128)(2,1)S(1)} %copy-done.5), kind=kOutput, calls=%fused_computation.69 | convolution fusion | flops 671088640 | bytes 7995392 | tf_op jit(solution)/shard_map/xcy,co->xoy/dot_general | solution.py:69
  12.6 1.8 %fusion.51 = f32[256,16,128]{2,0,1:T(8,128)} fusion(bf16[16,95,128]{2,0,1:T(8,128)(2,1)S(1)} %copy-done.6, bf16[95,256]{1,0:T(8,128)(2,1)S(1)} %copy-done.7), kind=kOutput, calls=%fused_computation.61 | convolution fusion | flops 99614720 | bytes 2534912 | tf_op jit(solution)/shard_map/sco,ch->sho/dot_general | solution.py:37
  14.4 2.6 %fusion.14 = bf16[10,256,642]{2,1,0:T(8,128)(2,1)S(1)} fusion(bf16[1,256,640]{2,1,0:T(8,128)(2,1)S(1)} %collective-permute-done.1, bf16[8,256,640]{2,1,0:T(8,128)(2,1)S(1)} %convert_bitcast_fusion, bf16[1,256,640]{2,1,0:T(8,128)(2,1)S(1)} %collective-permute-done), kind=kLoop, calls=%fused_computation.19 | loop fusion | flops 19722240 | bytes 6563840 | tf_op jit(solution)/shard_map/concatenate | solution.py:19
  17.0 3.5 %fusion.25 = f32[8,640,256]{1,2,0:T(8,128)} fusion(bf16[10,256,642]{2,1,0:T(8,128)(2,1)S(1)} %fusion.14, bf16[3,3,256,256]{3,2,1,0:T(8,128)(2,1)S(1)} %copy-done.5), kind=kOutput, calls=%fused_computation.31 | convolution fusion | flops 671088640 | bytes 7995392 | tf_op jit(solution)/shard_map/xcy,co->xoy/dot_general | solution.py:69
  20.6 3.5 %fusion.27 = f32[8,640,256]{1,2,0:T(8,128)} fusion(bf16[10,256,642]{2,1,0:T(8,128)(2,1)S(1)} %fusion.14, bf16[3,3,256,256]{3,2,1,0:T(8,128)(2,1)S(1)} %copy-done.5), kind=kOutput, calls=%fused_computation.33 | convolution fusion | flops 671088640 | bytes 7995392 | tf_op jit(solution)/shard_map/xcy,co->xoy/dot_general | solution.py:69
  24.1 3.2 %fusion.29 = f32[8,640,256]{1,2,0:T(8,128)} fusion(bf16[10,256,642]{2,1,0:T(8,128)(2,1)S(1)} %fusion.14, bf16[3,3,256,256]{3,2,1,0:T(8,128)(2,1)S(1)} %copy-done.5), kind=kOutput, calls=%fused_computation.35 | convolution fusion | flops 671088640 | bytes 7995392 | tf_op jit(solution)/shard_map/xcy,co->xoy/dot_general | solution.py:69
  27.3 3.7 %fusion.31 = f32[8,640,256]{1,2,0:T(8,128)} fusion(bf16[10,256,642]{2,1,0:T(8,128)(2,1)S(1)} %fusion.14, bf16[3,3,256,256]{3,2,1,0:T(8,128)(2,1)S(1)} %copy-done.5), kind=kOutput, calls=%fused_computation.37 | convolution fusion | flops 671088640 | bytes 7995392 | tf_op jit(solution)/shard_map/xcy,co->xoy/dot_general | solution.py:69
  31.0 3.2 %fusion.33 = f32[8,640,256]{1,2,0:T(8,128)} fusion(bf16[10,256,642]{2,1,0:T(8,128)(2,1)S(1)} %fusion.14, bf16[3,3,256,256]{3,2,1,0:T(8,128)(2,1)S(1)} %copy-done.5), kind=kOutput, calls=%fused_computation.39 | convolution fusion | flops 671088640 | bytes 7995392 | tf_op jit(solution)/shard_map/xcy,co->xoy/dot_general | solution.py:69
  34.2 3.2 %fusion.15 = f32[8,640,256]{1,2,0:T(8,128)} fusion(bf16[8,256,640]{2,1,0:T(8,128)(2,1)S(1)} %convert_bitcast_fusion, bf16[1,256,640]{2,1,0:T(8,128)(2,1)S(1)} %collective-permute-done, bf16[3,3,256,256]{3,2,1,0:T(8,128)(2,1)S(1)} %copy-done.5), kind=kOutput, calls=%fused_computation.21 | convolution fusion | flops 676986880 | bytes 8323072 | tf_op jit(solution)/shard_map/xcy,co->xoy/dot_general | solution.py:69
  37.4 3.2 %fusion.19 = f32[8,640,256]{1,2,0:T(8,128)} fusion(bf16[1,256,640]{2,1,0:T(8,128)(2,1)S(1)} %collective-permute-done.1, bf16[8,256,640]{2,1,0:T(8,128)(2,1)S(1)} %convert_bitcast_fusion, bf16[3,3,256,256]{3,2,1,0:T(8,128)(2,1)S(1)} %copy-done.5), kind=kOutput, calls=%fused_computation.25 | convolution fusion | flops 676986880 | bytes 8323072 | tf_op jit(solution)/shard_map/xcy,co->xoy/dot_general | solution.py:69
  40.6 17.7 %fusion.9 = bf16[8,256,640]{2,1,0:T(8,128)(2,1)} fusion(f32[8,640,256]{1,2,0:T(8,128)} %fusion.19, f32[8,640,256]{1,2,0:T(8,128)} %fusion.25, f32[8,640,256]{1,2,0:T(8,128)} %fusion.27, f32[8,640,256]{1,2,0:T(8,128)} %fusion.61, f32[8,640,256]{1,2,0:T(8,128)} %fusion.29, f32[8,640,256]{1,2,0:T(8,128)} %fusion.31, f32[8,640,256]{1,2,0:T(8,128)} %fusion.33, ...), kind=kOutput, calls=%fused_computation.13 | convolution fusion | flops 695992320 | bytes 49938432 | tf_op jit(solution)/shard_map/xcy,co->xoy/dot_general | solution.py:69
  58.3 2.2 %fusion.47 = bf16[8,16,640]{2,1,0:T(8,128)(2,1)S(1)} fusion(bf16[8,256,640]{2,1,0:T(8,128)(2,1)} %fusion.9, bf16[256,16]{0,1:T(8,128)(2,1)S(1)} %copy-done.8), kind=kOutput, calls=%fused_computation.54 | convolution fusion | flops 42024960 | bytes 2793472 | tf_op jit(solution)/shard_map/xhy,hf->xfy/dot_general | solution.py:76
  61.7 2.1 %collective-permute-start.4 = (bf16[16,128]{1,0:T(8,128)(2,1)S(1)}, bf16[16,128]{1,0:T(8,128)(2,1)S(1)}, u32[]{:S(2)}, u32[]{:S(2)}) collective-permute-start(bf16[16,128]{1,0:T(8,128)(2,1)S(1)} %squeeze.39), channel_id=1, source_target_pairs={{0,1},{1,0},{2,3},{3,2},{4,5},{5,4},{6,7},{7,6},{8,9},{9,8},{10,11... | collective-permute-start | bytes 12296 | tf_op jit(solution)/shard_map/ppermute | solution.py:30
  64.0 1.8 %copy.110 = bf16[40,16,8,16]{0,3,2,1:T(8,128)(2,1)S(1)} copy(bf16[40,16,8,16]{3,0,1,2:T(8,128)(2,1)} %bitcast.98) | data formatting | bytes 327680 | tf_op jit(solution)/shard_map/transpose | solution.py:83
  66.6 3.7 %collective-permute-start.3 = (bf16[1,40,16,128]{1,3,2,0:T(8,128)(2,1)S(1)}, bf16[1,40,16,128]{1,3,2,0:T(8,128)(2,1)}, u32[]{:S(2)}, u32[]{:S(2)}) collective-permute-start(bf16[1,40,16,128]{1,3,2,0:T(8,128)(2,1)S(1)} %bitcast.100), channel_id=1, source_target_pairs={{1,0},{2,1},{3,2},{4,3},{5,4},{6,5},{7,6},{8,7},{9,8},{10,9},{11,1... | collective-permute-start | bytes 491528 | tf_op jit(solution)/shard_map/ppermute | solution.py:18
  70.3 11.0 %collective-permute-done.5 = bf16[16,128]{1,0:T(8,128)(2,1)S(1)} collective-permute-done((bf16[16,128]{1,0:T(8,128)(2,1)S(1)}, bf16[16,128]{1,0:T(8,128)(2,1)S(1)}, u32[]{:S(2)}, u32[]{:S(2)}) %collective-permute-start.5) | collective-permute-done | bytes 4128 | tf_op jit(solution)/shard_map/ppermute | solution.py:30
  82.1 2.9 %collective-permute-done.6 = bf16[16,128]{1,0:T(8,128)(2,1)S(1)} collective-permute-done((bf16[16,128]{1,0:T(8,128)(2,1)S(1)}, bf16[16,128]{1,0:T(8,128)(2,1)S(1)}, u32[]{:S(2)}, u32[]{:S(2)}) %collective-permute-start.6) | collective-permute-done | bytes 4128 | tf_op jit(solution)/shard_map/ppermute | solution.py:30
  84.9 1.4 %collective-permute-start.7 = (bf16[16,128]{1,0:T(8,128)(2,1)S(1)}, bf16[16,128]{1,0:T(8,128)(2,1)S(1)}, u32[]{:S(2)}, u32[]{:S(2)}) collective-permute-start(bf16[16,128]{1,0:T(8,128)(2,1)S(1)} %collective-permute-done.6), channel_id=1, source_target_pairs={{0,8},{8,0},{1,9},{9,1},{2,10},{10,2},{3,11},{11,3},{4,12},{12,4},... | collective-permute-start | bytes 12296 | tf_op jit(solution)/shard_map/ppermute | solution.py:30
  86.3 1.3 %copy.111 = bf16[1,40,16,128]{3,2,1,0:T(8,128)(2,1)S(1)} copy(bf16[1,40,16,128]{1,3,2,0:T(8,128)(2,1)} %collective-permute-done.2) | data formatting | bytes 327680 | tf_op jit(solution)/shard_map/ppermute | solution.py:15
  87.6 1.3 %copy.113 = bf16[1,40,16,128]{3,2,1,0:T(8,128)(2,1)S(1)} copy(bf16[1,40,16,128]{1,3,2,0:T(8,128)(2,1)} %collective-permute-done.3) | data formatting | bytes 327680 | tf_op jit(solution)/shard_map/ppermute | solution.py:18
  90.2 3.6 %fusion.46 = bf16[16,256,128]{2,1,0:T(8,128)(2,1)} fusion(f32[256,16,128]{2,0,1:T(8,128)} %fusion.51, bf16[16,4,128,128]{3,2,1,0:T(8,128)(2,1)S(1)} %copy-done.3, bf16[16,4,16,128]{3,2,1,0:T(8,128)(2,1)S(1)} %bitcast.103, pred[16,4]{1,0:T(8,128)(4,1)S(1)} %copy.109, f32[16,128]{1,0:T(8,128)S(1)} %convert_reduce_fusion, bf16[16,256]{1,0:T(8,128)(2,1)S(1)} %copy-done.9), kind=kOutput, calls=%fused_computation.52 | convolution fusion | flops 51576832 | bytes 5521472 | tf_op jit(solution)/shard_map/sfo,fh->sho/dot_general | solution.py:39
  93.8 3.7 %fusion.50 = bf16[16,256,128]{2,1,0:T(8,128)(2,1)} fusion(bf16[16,256,128]{2,1,0:T(8,128)(2,1)} %fusion.46, pred[16]{0:T(512)(128)(4,1)S(1)} %broadcast_compare_fusion, bf16[256,256]{1,0:T(8,128)(2,1)S(1)} %copy-done.11), kind=kOutput, calls=%fused_computation.58 | convolution fusion | flops 274726912 | bytes 2228240 | tf_op jit(solution)/shard_map/sho,hk->sko/dot_general | solution.py:41
  (55 shorter events, 6.1 us)
Async XLA Ops:
  0.6 1.0 %copy-start = (bf16[8,48,640]{2,1,0:T(8,128)(2,1)S(1)}, bf16[8,48,640]{2,1,0:T(8,128)(2,1)}, u32[]{:S(2)}) copy-start(bf16[8,48,640]{2,1,0:T(8,128)(2,1)} %param.11) | copy-start | bytes 1474564
  0.6 8.3 %copy-start.5 = (bf16[3,3,256,256]{3,2,1,0:T(8,128)(2,1)S(1)}, bf16[3,3,256,256]{3,2,1,0:T(8,128)(2,1)}, u32[]{:S(2)}) copy-start(bf16[3,3,256,256]{3,2,1,0:T(8,128)(2,1)} %param.14) | copy-start | bytes 3538948
  3.3 11.1 %collective-permute-start = (bf16[1,256,640]{2,1,0:T(8,128)(2,1)S(1)}, bf16[1,256,640]{2,1,0:T(8,128)(2,1)S(1)}, u32[]{:S(2)}, u32[]{:S(2)}) collective-permute-start(bf16[1,256,640]{2,1,0:T(8,128)(2,1)S(1)} %get-tuple-element.2), channel_id=1, source_target_pairs={{0,1},{1,2},{2,3},{3,4},{4,5},{5,6},{6,7},{7,8},{8,9},{9,10},{10,1... | collective-permute-start | bytes 983048 | tf_op jit(solution)/shard_map/ppermute | solution.py:15
  3.8 10.6 %collective-permute-start.1 = (bf16[1,256,640]{2,1,0:T(8,128)(2,1)S(1)}, bf16[1,256,640]{2,1,0:T(8,128)(2,1)S(1)}, u32[]{:S(2)}, u32[]{:S(2)}) collective-permute-start(bf16[1,256,640]{2,1,0:T(8,128)(2,1)S(1)} %get-tuple-element.3), channel_id=1, source_target_pairs={{1,0},{2,1},{3,2},{4,3},{5,4},{6,5},{7,6},{8,7},{9,8},{10,9},{11,1... | collective-permute-start | bytes 983048 | tf_op jit(solution)/shard_map/ppermute | solution.py:18
  8.9 3.2 %copy-start.12 = (s32[16]{0:T(128)S(1)}, s32[16]{0:T(128)}, u32[]{:S(2)}) copy-start(s32[16]{0:T(128)} %param.21) | copy-start | bytes 196
  8.9 3.3 %copy-start.10 = (s32[16,3]{0,1:T(4,128)S(1)}, s32[16,3]{0,1:T(4,128)}, u32[]{:S(2)}) copy-start(s32[16,3]{0,1:T(4,128)} %param.20) | copy-start | bytes 580
  8.9 3.3 %copy-start.2 = (bf16[16,4,128,128]{3,2,1,0:T(8,128)(2,1)S(1)}, bf16[16,4,128,128]{3,2,1,0:T(8,128)(2,1)}, u32[]{:S(2)}) copy-start(bf16[16,4,128,128]{3,2,1,0:T(8,128)(2,1)} %param.19) | copy-start | bytes 6291460
  8.9 3.7 %copy-start.6 = (bf16[16,95,128]{2,0,1:T(8,128)(2,1)S(1)}, bf16[16,95,128]{2,0,1:T(8,128)(2,1)}, u32[]{:S(2)}) copy-start(bf16[16,95,128]{2,0,1:T(8,128)(2,1)} %param.12) | copy-start | bytes 1167364
  8.9 3.7 %copy-start.7 = (bf16[95,256]{1,0:T(8,128)(2,1)S(1)}, bf16[95,256]{1,0:T(8,128)(2,1)}, u32[]{:S(2)}) copy-start(bf16[95,256]{1,0:T(8,128)(2,1)} %param.16) | copy-start | bytes 145924
  17.0 13.9 %copy-start.1 = (bf16[10,256,642]{2,1,0:T(8,128)(2,1)}, bf16[10,256,642]{2,1,0:T(8,128)(2,1)S(1)}, u32[]{:S(2)}) copy-start(bf16[10,256,642]{2,1,0:T(8,128)(2,1)S(1)} %fusion.14) | copy-start | bytes 9861124
  40.6 17.7 %copy-start.8 = (bf16[256,16]{0,1:T(8,128)(2,1)S(1)}, bf16[256,16]{0,1:T(8,128)(2,1)}, u32[]{:S(2)}) copy-start(bf16[256,16]{0,1:T(8,128)(2,1)} %param.15) | copy-start | bytes 24580
  61.5 2.4 %copy-start.4 = (bf16[8,16,40,16]{3,2,1,0:T(8,128)(2,1)}, bf16[8,16,40,16]{3,2,1,0:T(8,128)(2,1)S(1)}, u32[]{:S(2)}) copy-start(bf16[8,16,40,16]{3,2,1,0:T(8,128)(2,1)S(1)} %reshape.26) | copy-start | bytes 491524
  61.7 8.6 %collective-permute-start.4 = (bf16[16,128]{1,0:T(8,128)(2,1)S(1)}, bf16[16,128]{1,0:T(8,128)(2,1)S(1)}, u32[]{:S(2)}, u32[]{:S(2)}) collective-permute-start(bf16[16,128]{1,0:T(8,128)(2,1)S(1)} %squeeze.39), channel_id=1, source_target_pairs={{0,1},{1,0},{2,3},{3,2},{4,5},{5,4},{6,7},{7,6},{8,9},{9,8},{10,11... | collective-permute-start | bytes 12296 | tf_op jit(solution)/shard_map/ppermute | solution.py:30
  64.0 26.2 %copy-start.3 = (bf16[16,4,128,128]{3,2,1,0:T(8,128)(2,1)S(1)}, bf16[16,4,128,128]{3,2,1,0:T(8,128)(2,1)}, u32[]{:S(2)}) copy-start(bf16[16,4,128,128]{3,2,1,0:T(8,128)(2,1)} %param.19) | copy-start | bytes 6291460
  64.0 26.2 %copy-start.9 = (bf16[16,256]{1,0:T(8,128)(2,1)S(1)}, bf16[16,256]{1,0:T(8,128)(2,1)}, u32[]{:S(2)}) copy-start(bf16[16,256]{1,0:T(8,128)(2,1)} %param.17) | copy-start | bytes 24580
  65.8 20.5 %collective-permute-start.2 = (bf16[1,40,16,128]{1,3,2,0:T(8,128)(2,1)S(1)}, bf16[1,40,16,128]{1,3,2,0:T(8,128)(2,1)}, u32[]{:S(2)}, u32[]{:S(2)}) collective-permute-start(bf16[1,40,16,128]{1,3,2,0:T(8,128)(2,1)S(1)} %bitcast.99), channel_id=1, source_target_pairs={{0,1},{1,2},{2,3},{3,4},{4,5},{5,6},{6,7},{7,8},{8,9},{9,10},{10,1... | collective-permute-start | bytes 491528 | tf_op jit(solution)/shard_map/ppermute | solution.py:15
  66.6 21.0 %collective-permute-start.3 = (bf16[1,40,16,128]{1,3,2,0:T(8,128)(2,1)S(1)}, bf16[1,40,16,128]{1,3,2,0:T(8,128)(2,1)}, u32[]{:S(2)}, u32[]{:S(2)}) collective-permute-start(bf16[1,40,16,128]{1,3,2,0:T(8,128)(2,1)S(1)} %bitcast.100), channel_id=1, source_target_pairs={{1,0},{2,1},{3,2},{4,3},{5,4},{6,5},{7,6},{8,7},{9,8},{10,9},{11,1... | collective-permute-start | bytes 491528 | tf_op jit(solution)/shard_map/ppermute | solution.py:18
  70.3 11.0 %collective-permute-start.5 = (bf16[16,128]{1,0:T(8,128)(2,1)S(1)}, bf16[16,128]{1,0:T(8,128)(2,1)S(1)}, u32[]{:S(2)}, u32[]{:S(2)}) collective-permute-start(bf16[16,128]{1,0:T(8,128)(2,1)S(1)} %collective-permute-done.4), channel_id=1, source_target_pairs={{0,2},{2,0},{1,3},{3,1},{4,6},{6,4},{5,7},{7,5},{8,10},{10,8},{9,1... | collective-permute-start | bytes 12296 | tf_op jit(solution)/shard_map/ppermute | solution.py:30
  81.3 3.6 %collective-permute-start.6 = (bf16[16,128]{1,0:T(8,128)(2,1)S(1)}, bf16[16,128]{1,0:T(8,128)(2,1)S(1)}, u32[]{:S(2)}, u32[]{:S(2)}) collective-permute-start(bf16[16,128]{1,0:T(8,128)(2,1)S(1)} %collective-permute-done.5), channel_id=1, source_target_pairs={{0,4},{4,0},{1,5},{5,1},{2,6},{6,2},{3,7},{7,3},{8,12},{12,8},{9,1... | collective-permute-start | bytes 12296 | tf_op jit(solution)/shard_map/ppermute | solution.py:30
  84.9 4.5 %collective-permute-start.7 = (bf16[16,128]{1,0:T(8,128)(2,1)S(1)}, bf16[16,128]{1,0:T(8,128)(2,1)S(1)}, u32[]{:S(2)}, u32[]{:S(2)}) collective-permute-start(bf16[16,128]{1,0:T(8,128)(2,1)S(1)} %collective-permute-done.6), channel_id=1, source_target_pairs={{0,8},{8,0},{1,9},{9,1},{2,10},{10,2},{3,11},{11,3},{4,12},{12,4},... | collective-permute-start | bytes 12296 | tf_op jit(solution)/shard_map/ppermute | solution.py:30
  90.1 3.6 %copy-start.11 = (bf16[256,256]{1,0:T(8,128)(2,1)S(1)}, bf16[256,256]{1,0:T(8,128)(2,1)}, u32[]{:S(2)}) copy-start(bf16[256,256]{1,0:T(8,128)(2,1)} %param.18) | copy-start | bytes 393220
where the time goes:
time: 97.8 us; the launch traced here: 97.4 us
  matrix products  57.3 us (59%)
  waiting for transfers between devices  14.4 us (15%)
  starting transfers between devices  13.9 us (14%)
  local copies, waits for them, and re-layouts  7.75 us (8%)
  other arithmetic  3.18 us (3%)
    dot_general x9, matrix products, per_device(): jnp.einsum('xcy,co->xoy', padded[shift_x:shift_x + columns, :, shift_y:sh...  44.4 us
    ppermute x4, waiting for transfers between devices, partner(): return lax.ppermute(block, axis, route)  14.4 us
    ppermute x2, starting transfers between devices, with_halo(): lax.ppermute(lax.slice_in_dim(block, 0, width, axis=dim), axis, backward)  8.74 us
    ppermute x4, starting transfers between devices, partner(): return lax.ppermute(block, axis, route)  3.86 us
    dot_general x1, matrix products, encode_ocean(): jnp.einsum('sho,hk->sko', base, mix_weight, preferred_element_type=jnp.fl...  3.67 us
    dot_general x1, matrix products, encode_ocean(): jnp.einsum('sfo,fh->sho', regrid, couple_weight, preferred_element_type=j...  3.6 us
    concatenate x2, other arithmetic, with_halo(): block = jnp.concatenate([low, block, high], axis=dim)  2.68 us
    dot_general x1, matrix products, per_device(): jnp.einsum('xhy,hf->xfy', atm_hidden, flux_weight, preferred_element_type...  2.19 us
  transfers between devices with their start and end apart: 8, of which 3 were waited for; matrix products, arithmetic and copies ran while one was open for 11% of the time, Pallas kernels for 0%

commit v1 on v0

v1 whole, which is shorter than its diff:
```python
import functools

import jax
import jax.numpy as jnp
from jax import lax
from jax.experimental import pallas as pl
from jax.experimental.pallas import tpu as pltpu
from jax.sharding import PartitionSpec as P

TLAT = 16
FOLDB = 2
LANES = 128
MESH = pl.DeviceIdType.MESH
F32 = jnp.float32
BF16 = jnp.bfloat16


def gelu(z):
    return 0.5 * z * (1.0 + jnp.tanh(0.7978845608028654 * (z + 0.044715 * z * z * z)))


def dot(a, b):
    return jnp.dot(a, b, preferred_element_type=F32)


def regroup(blocks, tlat):
    count = len(blocks)
    group = lax.broadcasted_iota(jnp.int32, blocks[0].shape, 1) // tlat
    step = count // 2
    while step:
        low = (group // step) % 2 == 0
        out = list(blocks)
        for i in range(count):
            if (i // step) % 2 == 0:
                first, second = blocks[i], blocks[i + step]
                out[i] = jnp.where(low, first, pltpu.roll(second, step * tlat, 1))
                out[i + step] = jnp.where(low, pltpu.roll(first, LANES - step * tlat, 1), second)
        blocks = out
        step //= 2
    return blocks


def kernel(
    strips,
    pair_ref, mask_ref, atm_hbm, ocean_hbm, lift_ref, conv_hbm, flux_ref, ow_ref, cw_ref, mix_ref, regrid_hbm,
    hid_hbm, oce_hbm,
    xin, conv_v, ocean_v, regrid_v, col, folded_f, wt, lt, ocean_f, wocean, mixt, table, mirror, hid, ustate, oce,
    load_sem, regrid_sem, halo_send, halo_recv, flux_send, flux_recv, mir_sem, hid_sem, oce_sem,
):
    columns, channels, lat = atm_hbm.shape
    width = lift_ref.shape[1]
    och = ow_ref.shape[0]
    fl = flux_ref.shape[0]
    tiles = ocean_hbm.shape[1]
    chunks = lat // LANES
    per = LANES // TLAT
    stride = 3 * channels
    depth = wt.shape[1]

    me = lax.axis_index("lon")
    right = lax.rem(me + 1, strips)
    left = lax.rem(me + strips - 1, strips)
    fold = strips - 1 - me

    def remote(src, dst, send, recv, to):
        return pltpu.make_async_remote_copy(
            src_ref=src, dst_ref=dst, send_sem=send, recv_sem=recv, device_id={"lon": to}, device_id_type=MESH
        )

    barrier = pltpu.get_barrier_semaphore()
    for other in (left, right, fold):
        pl.semaphore_signal(barrier, inc=1, device_id={"lon": other}, device_id_type=MESH)

    load_atm = pltpu.make_async_copy(atm_hbm, xin.at[pl.ds(1, columns)], load_sem.at[0])
    load_conv = pltpu.make_async_copy(conv_hbm, conv_v, load_sem.at[1])
    load_ocean = pltpu.make_async_copy(ocean_hbm, ocean_v, load_sem.at[2])
    load_atm.start()
    load_conv.start()
    load_ocean.start()
    load_main = pltpu.make_async_copy(
        regrid_hbm.at[:, pl.ds(0, 3)], regrid_v.at[:, pl.ds(0, 3)], regrid_sem.at[0]
    )
    load_fold = pltpu.make_async_copy(
        regrid_hbm.at[pl.ds(tiles - FOLDB, FOLDB), pl.ds(3, 1)],
        regrid_v.at[pl.ds(tiles - FOLDB, FOLDB), pl.ds(3, 1)],
        regrid_sem.at[1],
    )
    load_main.start()
    load_fold.start()

    pl.semaphore_wait(barrier, 3)
    halo_r = remote(atm_hbm.at[columns - 1], xin.at[0], halo_send.at[0], halo_recv.at[0], right)
    halo_l = remote(atm_hbm.at[0], xin.at[columns + 1], halo_send.at[1], halo_recv.at[1], left)
    halo_r.start()
    halo_l.start()

    lt[...] = lift_ref[...].astype(F32).T.astype(BF16)
    mixt[...] = mix_ref[...].astype(F32).T.astype(BF16)
    joined = jnp.concatenate(
        [
            ow_ref[...].astype(F32),
            jnp.zeros((96 - och, width), F32),
            cw_ref[...].astype(F32),
            jnp.zeros((LANES - 96 - fl, width), F32),
        ],
        axis=0,
    )
    wocean[...] = joined.T.astype(BF16)

    tail = col.shape[1] - (columns + 1) * stride
    for c in range(chunks):
        col[c, (columns + 1) * stride :, :] = jnp.zeros((tail, LANES), BF16)

    def spread(x):
        v = xin[x].astype(F32)
        lane = lax.broadcasted_iota(jnp.int32, v.shape, 1)
        south = jnp.where(lane == 0, 0.0, pltpu.roll(v, 1, 1))
        north = jnp.where(lane == lat - 1, 0.0, pltpu.roll(v, lat - 1, 1))
        for b, piece in enumerate((south, v, north)):
            piece = piece.astype(BF16)
            rows = pl.ds(pl.multiple_of(x * stride + b * channels, 16), channels)
            for c in range(chunks):
                col[c, rows, :] = piece[:, c * LANES : (c + 1) * LANES]

    load_atm.wait()

    def own(x, carry):
        spread(x + 1)
        return carry

    lax.fori_loop(0, columns, own, 0)

    load_conv.wait()
    for k in range(9):
        folded_f[k * channels : (k + 1) * channels, :] = dot(lift_ref[...], conv_v[k // 3, k % 3])
    folded_f[9 * channels :, :] = jnp.zeros((depth - 9 * channels, width), F32)
    wt[...] = folded_f[...].T.astype(BF16)

    load_ocean.wait()
    ocean_f[...] = ocean_v[...].astype(F32).reshape(ocean_f.shape)
    for t in range(tiles):
        ustate[t, 80:, :] = jnp.zeros((ustate.shape[1] - 80, LANES), BF16)
        ustate[t, 0:och, :] = ocean_f[pl.ds(t, och, stride=tiles), :].astype(BF16)

    halo_r.wait()
    halo_l.wait()
    spread(0)
    spread(columns + 1)

    def flux_copy(c, to, side, index):
        rows = pl.ds(c * per, per)
        return remote(
            table.at[1, rows], table.at[side, rows], flux_send.at[c, index], flux_recv.at[c, index], to
        )

    def hid_copy(c):
        return pltpu.make_async_copy(
            hid.at[c], hid_hbm.at[:, :, pl.ds(pl.multiple_of(c * LANES, LANES), LANES)], hid_sem.at[c]
        )

    to_fold = remote(table.at[1, chunks * per - 1], mirror, mir_sem.at[0], mir_sem.at[1], fold)

    def chunk(i, carry):
        c = chunks - 1 - i
        flux = []
        for x in range(0, columns, 2):
            rhs = jnp.concatenate(
                [col[c, x * stride : x * stride + depth, :], col[c, (x + 1) * stride : (x + 1) * stride + depth, :]],
                axis=1,
            )
            at = (x + 1) * stride + channels
            mid = jnp.concatenate(
                [col[c, at : at + channels, :], col[c, at + stride : at + stride + channels, :]], axis=1
            )
            conv = dot(wt[...], rhs)
            lifted = dot(lt[...], mid).astype(BF16).astype(F32)
            hidden = (lifted + gelu(conv)).astype(BF16)
            hid[c, x] = hidden[:, :LANES]
            hid[c, x + 1] = hidden[:, LANES:]
            f = dot(flux_ref[...], hidden)
            flux += [f[:, :LANES], f[:, LANES:]]
        hid_copy(c).start()
        for a, tile in enumerate(regroup(flux, TLAT)):
            table[1, c * per + a] = tile.astype(BF16)
        flux_copy(c, right, 0, 0).start()
        flux_copy(c, left, 2, 1).start()

        @pl.when(i == 0)
        def _():
            to_fold.start()

        return carry

    lax.fori_loop(0, chunks, chunk, 0)

    load_main.wait()
    load_fold.wait()

    def arrive(c, carry):
        flux_copy(c, right, 0, 0).wait()
        flux_copy(c, left, 2, 1).wait()
        return carry

    lax.fori_loop(0, chunks, arrive, 0)
    to_fold.wait()

    ones = jnp.ones((fl, LANES), BF16)
    mirrored = mirror[...]

    def regrid(t, folded):
        got = [table[p, pair_ref[p, t]] for p in range(3)]
        weights = [regrid_v[t, p] for p in range(3)]
        if folded:
            got.append(mirrored)
            weights.append(regrid_v[t, 3])
        lhs = jnp.concatenate([jnp.concatenate([g, ones], axis=0) for g in got], axis=1)
        rhs = jnp.concatenate(weights, axis=1)
        sums = lax.dot_general(lhs, rhs, (((1,), (1,)), ((), ())), preferred_element_type=F32)
        ustate[t, 96 : 96 + fl, :] = (sums[:fl] / sums[fl : fl + 1]).astype(BF16)

    def encode(t):
        rhs = jnp.concatenate([ustate[t], ustate[t + 1]], axis=1)
        base = dot(wocean[...], rhs).astype(BF16)
        mixed = dot(mixt[...], base)
        result = (base.astype(F32) + gelu(mixed)).astype(BF16)
        for k in range(2):
            water = jnp.full((width, LANES), mask_ref[t + k], jnp.int32) == 1
            oce[t + k] = jnp.where(water, result[:, k * LANES : (k + 1) * LANES].astype(F32), 0.0).astype(BF16)

    def oce_copy(t, index):
        return pltpu.make_async_copy(oce.at[pl.ds(t, 4)], oce_hbm.at[pl.ds(t, 4)], oce_sem.at[index])

    for t in range(tiles):
        regrid(t, t >= tiles - FOLDB)

    for t in range(0, tiles, 2):
        encode(t)
        if t % 4 == 2:
            oce_copy(t - 2, t // 4).start()
    for t in range(0, tiles, 4):
        oce_copy(t, t // 4).wait()

    def leave(c, carry):
        hid_copy(c).wait()
        return carry

    lax.fori_loop(0, chunks, leave, 0)


def per_device(
    strips,
    atm_in,
    ocean_in,
    lift_weight,
    conv_weight,
    flux_weight,
    ocean_weight,
    couple_weight,
    mix_weight,
    regrid_weight,
    pair_tile,
    ocean_mask,
):
    columns, channels, lat = atm_in.shape
    width = lift_weight.shape[1]
    fl = flux_weight.shape[1]
    tiles, och, cells = ocean_in.shape
    chunks = lat // LANES
    stride = 3 * channels
    depth = -(-9 * channels // 256) * 256
    rows = (columns - 1) * stride + depth
    hbm = pl.BlockSpec(memory_space=pl.ANY)
    vmem = pl.BlockSpec(memory_space=pltpu.VMEM)
    smem = pl.BlockSpec(memory_space=pltpu.SMEM)
    dma = pltpu.SemaphoreType.DMA
    flops = 2 * columns * lat * width * (12 * channels) + 2 * tiles * cells * width * (width + 128)
    return pl.pallas_call(
        functools.partial(kernel, strips),
        out_shape=(
            jax.ShapeDtypeStruct((columns, width, lat), BF16),
            jax.ShapeDtypeStruct((tiles, width, cells), BF16),
        ),
        in_specs=[smem, smem, hbm, hbm, vmem, hbm, vmem, vmem, vmem, vmem, hbm],
        out_specs=(hbm, hbm),
        scratch_shapes=[
            pltpu.VMEM((columns + 2, channels, lat), BF16),
            pltpu.VMEM(conv_weight.shape, BF16),
            pltpu.VMEM((och, tiles, cells), BF16),
            pltpu.VMEM(regrid_weight.shape, BF16),
            pltpu.VMEM((chunks, rows, LANES), BF16),
            pltpu.VMEM((depth, width), F32),
            pltpu.VMEM((width, depth), BF16),
            pltpu.VMEM((width, channels), BF16),
            pltpu.VMEM((och * tiles, cells), F32),
            pltpu.VMEM((width, LANES), BF16),
            pltpu.VMEM((width, width), BF16),
            pltpu.VMEM((3, lat // TLAT, fl, LANES), BF16),
            pltpu.VMEM((fl, LANES), BF16),
            pltpu.VMEM((chunks, columns, width, LANES), BF16),
            pltpu.VMEM((tiles, LANES, cells), BF16),
            pltpu.VMEM((tiles, width, cells), BF16),
            dma((3,)),
            dma((2,)),
            dma((2,)),
            dma((2,)),
            dma((chunks, 2)),
            dma((chunks, 2)),
            dma((2,)),
            dma((chunks,)),
            dma((tiles // 4,)),
        ],
        compiler_params=pltpu.CompilerParams(
            collective_id=0, has_side_effects=True, vmem_limit_bytes=56 * 1024 * 1024
        ),
        cost_estimate=pl.CostEstimate(flops=flops, bytes_accessed=8 * 1024 * 1024, transcendentals=2 * 1024 * 1024),
    )(
        pair_tile.T, ocean_mask, atm_in, ocean_in.transpose(1, 0, 2), lift_weight, conv_weight,
        flux_weight.T, ocean_weight, couple_weight, mix_weight, regrid_weight,
    )


def solution(mesh):
    in_specs = (
        P(("groups", "lon"), None, None),
        P(("groups", "lon"), None, None),
        P(),
        P(),
        P(),
        P(),
        P(),
        P(),
        P("lon", None, None, None),
        P("lon", None),
        P("lon"),
    )
    out_specs = (P(("groups", "lon"), None, None), P(("groups", "lon"), None, None))
    return jax.shard_map(
        functools.partial(per_device, mesh.shape["lon"]),
        mesh=mesh,
        in_specs=in_specs,
        out_specs=out_specs,
        check_vma=False,
    )
```

time: 97.8 us -> 29.4 us (0.30)
  matrix products: 57.3 us -> 0 us
  Pallas kernels: 0 us -> 24 us
  waiting for transfers between devices: 14.4 us -> 0 us
  starting transfers between devices: 13.9 us -> 0 us
  other arithmetic: 3.18 us -> 0 us
  local copies, waits for them, and re-layouts: 7.75 us -> 4.57 us
    dot_general x14 -> x0, matrix products: 57.3 us -> none  [the longest x9 44.4 us: per_device(): jnp.einsum('xcy,co->xoy', padded[shift_x:shift_x + columns, :, shift_y:sh...]
    pallas_call x0 -> x1, Pallas kernels: none -> 24 us  [per_device(): pl.pallas_call(functools.partial(kernel, strips), out_shape=(jax.ShapeDty...]
    ppermute x8 -> x0, waiting for transfers between devices: 14.4 us -> none  [the longest x4 14.4 us: partner(): return lax.ppermute(block, axis, route)]
    ppermute x8 -> x0, starting transfers between devices: 13.9 us -> none  [the longest x2 8.74 us: with_halo(): lax.ppermute(lax.slice_in_dim(block, 0, width, axis=dim), axis, backward)]
    unnamed x26 -> x4, local copies, waits for them, and re-layouts: 1.08 us -> 4.57 us
    concatenate x3 -> x0, other arithmetic: 2.73 us -> none  [the longest x2 2.68 us: with_halo(): block = jnp.concatenate([low, block, high], axis=dim)]
    ppermute x2 -> x0, local copies, waits for them, and re-layouts: 2.54 us -> none  [the longest x1 1.27 us: with_halo(): lax.ppermute(lax.slice_in_dim(block, 0, width, axis=dim), axis, backward)]
    transpose x1 -> x0, local copies, waits for them, and re-layouts: 1.8 us -> none  [per_device(): tiles = flux.reshape(columns, flux_count, tiles_lat, TLAT).transpose(2, 1...]
  transfers between devices with their start and end apart: 8 -> 0, of which waited for: 3 -> 0; matrix products, arithmetic and copies ran while one was open for 11% -> 0% of each run, Pallas kernels for 0% -> 0%
where the time goes in v1:
time: 29.4 us; the launch traced here: 29.3 us
  Pallas kernels  24 us (82%)
  local copies, waits for them, and re-layouts  4.57 us (16%)
  between operations  0.65 us (2%)
    pallas_call x1, Pallas kernels, per_device(): pl.pallas_call(functools.partial(kernel, strips), out_shape=(jax.ShapeDty...  24 us
    unnamed x4, local copies, waits for them, and re-layouts  4.57 us

profile of v1, /device:TPU:0, one launch (start us, length us, event | category | flops | bytes accessed | tf_op | source)
XLA Modules:
  0.0 29.3 jit_solution(12426847232131116218)
XLA Ops:
  0.6 24.0 %shard_map.122 = (bf16[8,256,640]{2,1,0:T(8,128)(2,1)}, bf16[16,256,128]{2,1,0:T(8,128)(2,1)}) custom-call(s32[3,16]{1,0:T(4,128)} %bitcast.5, s32[16]{0:T(128)} %mask_ref.1, bf16[8,48,640]{2,1,0:T(8,128)(2,1)} %atm_hbm.1, bf16[95,16,128]{2,1,0:T(8,128)(2,1)} %bitcast.3, bf16[48,256]{1,0:T(8,128)(2,1)} %lift_ref.1, bf16[3,3,256,256]{3,2,1,0:T(8,128)(2,1)} %conv_hbm.1, ...), custom_call_target="tpu_custom_call" | custom-call | flops 1912602624 | bytes 8388608 | tf_op jit(solution)/shard_map/pallas_call | solution.py:277
  24.7 0.0 copy-start
  24.7 3.6 %copy.15 = bf16[8,256,640]{2,1,0:T(8,128)(2,1)} copy(bf16[8,256,640]{2,1,0:T(8,128)(2,1)} %get-tuple-element.4) | data formatting | bytes 5242880
  28.3 0.0 copy-done
  28.3 1.0 %copy.16 = bf16[16,256,128]{2,1,0:T(8,128)(2,1)} copy(bf16[16,256,128]{2,1,0:T(8,128)(2,1)S(1)} %copy-done) | data formatting | bytes 2097152
Async XLA Ops:
  24.7 3.6 %copy-start = (bf16[16,256,128]{2,1,0:T(8,128)(2,1)S(1)}, bf16[16,256,128]{2,1,0:T(8,128)(2,1)}, u32[]{:S(2)}) copy-start(bf16[16,256,128]{2,1,0:T(8,128)(2,1)} %get-tuple-element.5) | copy-start | bytes 3145732

commit v2 on v1

--- a/solution.py
+++ b/solution.py
@@ -9,6 +9,7 @@
 
 TLAT = 16
 FOLDB = 2
+MAXACT = 8
 LANES = 128
 MESH = pl.DeviceIdType.MESH
 F32 = jnp.float32
@@ -40,18 +41,24 @@
     return blocks
 
 
+def tally(mask, count):
+    ahead = [jnp.int32(0)]
+    for t in range(count - 1):
+        ahead.append(ahead[-1] + mask[t])
+    return ahead
+
+
 def kernel(
     strips,
-    pair_ref, mask_ref, atm_hbm, ocean_hbm, lift_ref, conv_hbm, flux_ref, ow_ref, cw_ref, mix_ref, regrid_hbm,
-    hid_hbm, oce_hbm,
-    xin, conv_v, ocean_v, regrid_v, col, folded_f, wt, lt, ocean_f, wocean, mixt, table, mirror, hid, ustate, oce,
-    load_sem, regrid_sem, halo_send, halo_recv, flux_send, flux_recv, mir_sem, hid_sem, oce_sem,
+    pair_hbm, mask_hbm, atm_hbm, ocean_hbm, lift_hbm, conv_hbm, flux_hbm, regrid_hbm,
+    hid_out, packed_out,
+    pair_ref, mask_ref, lift_ref, flux_ref, xin, conv_v, ocean_v, regrid_v, col, folded_f, wt, lt, ocean_f, ustate, packed, table, mirror, hid,
+    load_sem, regrid_sem, halo_send, halo_recv, flux_send, flux_recv, mir_sem, hid_sem, packed_sem,
 ):
     columns, channels, lat = atm_hbm.shape
     width = lift_ref.shape[1]
-    och = ow_ref.shape[0]
+    och, tiles = ocean_hbm.shape[:2]
     fl = flux_ref.shape[0]
-    tiles = ocean_hbm.shape[1]
     chunks = lat // LANES
     per = LANES // TLAT
     stride = 3 * channels
@@ -74,9 +81,6 @@
     load_atm = pltpu.make_async_copy(atm_hbm, xin.at[pl.ds(1, columns)], load_sem.at[0])
     load_conv = pltpu.make_async_copy(conv_hbm, conv_v, load_sem.at[1])
     load_ocean = pltpu.make_async_copy(ocean_hbm, ocean_v, load_sem.at[2])
-    load_atm.start()
-    load_conv.start()
-    load_ocean.start()
     load_main = pltpu.make_async_copy(
         regrid_hbm.at[:, pl.ds(0, 3)], regrid_v.at[:, pl.ds(0, 3)], regrid_sem.at[0]
     )
@@ -85,31 +89,30 @@
         regrid_v.at[pl.ds(tiles - FOLDB, FOLDB), pl.ds(3, 1)],
         regrid_sem.at[1],
     )
-    load_main.start()
-    load_fold.start()
+    smalls = [
+        pltpu.make_async_copy(source, target, load_sem.at[3 + i])
+        for i, (source, target) in enumerate(
+            ((lift_hbm, lift_ref), (flux_hbm, flux_ref), (pair_hbm, pair_ref), (mask_hbm, mask_ref))
+        )
+    ]
+    smalls[0].start()
+    load_atm.start()
+    load_conv.start()
+    for small in smalls[1:]:
+        small.start()
+
+    smalls[0].wait()
+    lt[...] = lift_ref[...].astype(F32).T.astype(BF16)
+    tail = col.shape[1] - (columns + 1) * stride
+    for c in range(chunks):
+        col[c, (columns + 1) * stride :, :] = jnp.zeros((tail, LANES), BF16)
+    folded_f[9 * channels :, :] = jnp.zeros((depth - 9 * channels, width), F32)
 
     pl.semaphore_wait(barrier, 3)
     halo_r = remote(atm_hbm.at[columns - 1], xin.at[0], halo_send.at[0], halo_recv.at[0], right)
     halo_l = remote(atm_hbm.at[0], xin.at[columns + 1], halo_send.at[1], halo_recv.at[1], left)
     halo_r.start()
     halo_l.start()
-
-    lt[...] = lift_ref[...].astype(F32).T.astype(BF16)
-    mixt[...] = mix_ref[...].astype(F32).T.astype(BF16)
-    joined = jnp.concatenate(
-        [
-            ow_ref[...].astype(F32),
-            jnp.zeros((96 - och, width), F32),
-            cw_ref[...].astype(F32),
-            jnp.zeros((LANES - 96 - fl, width), F32),
-        ],
-        axis=0,
-    )
-    wocean[...] = joined.T.astype(BF16)
-
-    tail = col.shape[1] - (columns + 1) * stride
-    for c in range(chunks):
-        col[c, (columns + 1) * stride :, :] = jnp.zeros((tail, LANES), BF16)
 
     def spread(x):
         v = xin[x].astype(F32)
@@ -118,29 +121,22 @@
         north = jnp.where(lane == lat - 1, 0.0, pltpu.roll(v, lat - 1, 1))
         for b, piece in enumerate((south, v, north)):
             piece = piece.astype(BF16)
-            rows = pl.ds(pl.multiple_of(x * stride + b * channels, 16), channels)
+            at = x * stride + b * channels
             for c in range(chunks):
-                col[c, rows, :] = piece[:, c * LANES : (c + 1) * LANES]
+                col[c, at : at + channels, :] = piece[:, c * LANES : (c + 1) * LANES]
 
     load_atm.wait()
-
-    def own(x, carry):
-        spread(x + 1)
-        return carry
-
-    lax.fori_loop(0, columns, own, 0)
-
     load_conv.wait()
+    load_ocean.start()
+    load_main.start()
+    load_fold.start()
+    for small in smalls[1:]:
+        small.wait()
     for k in range(9):
         folded_f[k * channels : (k + 1) * channels, :] = dot(lift_ref[...], conv_v[k // 3, k % 3])
-    folded_f[9 * channels :, :] = jnp.zeros((depth - 9 * channels, width), F32)
+        if k < columns:
+            spread(k + 1)
     wt[...] = folded_f[...].T.astype(BF16)
-
-    load_ocean.wait()
-    ocean_f[...] = ocean_v[...].astype(F32).reshape(ocean_f.shape)
-    for t in range(tiles):
-        ustate[t, 80:, :] = jnp.zeros((ustate.shape[1] - 80, LANES), BF16)
-        ustate[t, 0:och, :] = ocean_f[pl.ds(t, och, stride=tiles), :].astype(BF16)
 
     halo_r.wait()
     halo_l.wait()
@@ -155,7 +151,7 @@
 
     def hid_copy(c):
         return pltpu.make_async_copy(
-            hid.at[c], hid_hbm.at[:, :, pl.ds(pl.multiple_of(c * LANES, LANES), LANES)], hid_sem.at[c]
+            hid.at[c], hid_out.at[:, :, pl.ds(pl.multiple_of(c * LANES, LANES), LANES)], hid_sem.at[c]
         )
 
     to_fold = remote(table.at[1, chunks * per - 1], mirror, mir_sem.at[0], mir_sem.at[1], fold)
@@ -193,6 +189,24 @@
 
     lax.fori_loop(0, chunks, chunk, 0)
 
+    load_ocean.wait()
+    ocean_f[...] = ocean_v[...].astype(F32).reshape(ocean_f.shape)
+    for t in range(tiles):
+        ustate[t, 80:, :] = jnp.zeros((ustate.shape[1] - 80, LANES), BF16)
+        ustate[t, 0:och, :] = ocean_f[pl.ds(t, och, stride=tiles), :].astype(BF16)
+
+    plain = tiles - FOLDB
+    ahead = tally(mask_ref, plain)
+    slots = []
+    for k in range(MAXACT - FOLDB):
+        slot = jnp.int32(0)
+        for t in range(k, plain):
+            slot = jnp.where((mask_ref[t] == 1) & (ahead[t] == k), t, slot)
+        slots.append(slot)
+    slots += [plain + k for k in range(FOLDB)]
+    for k, t in enumerate(slots):
+        packed[k // 2, :, (k % 2) * LANES : (k % 2 + 1) * LANES] = ustate[t]
+
     load_main.wait()
     load_fold.wait()
 
@@ -206,45 +220,74 @@
 
     ones = jnp.ones((fl, LANES), BF16)
     mirrored = mirror[...]
-
-    def regrid(t, folded):
+    for k, t in enumerate(slots):
         got = [table[p, pair_ref[p, t]] for p in range(3)]
         weights = [regrid_v[t, p] for p in range(3)]
-        if folded:
+        if k >= MAXACT - FOLDB:
             got.append(mirrored)
             weights.append(regrid_v[t, 3])
         lhs = jnp.concatenate([jnp.concatenate([g, ones], axis=0) for g in got], axis=1)
         rhs = jnp.concatenate(weights, axis=1)
         sums = lax.dot_general(lhs, rhs, (((1,), (1,)), ((), ())), preferred_element_type=F32)
-        ustate[t, 96 : 96 + fl, :] = (sums[:fl] / sums[fl : fl + 1]).astype(BF16)
-
-    def encode(t):
-        rhs = jnp.concatenate([ustate[t], ustate[t + 1]], axis=1)
-        base = dot(wocean[...], rhs).astype(BF16)
-        mixed = dot(mixt[...], base)
-        result = (base.astype(F32) + gelu(mixed)).astype(BF16)
-        for k in range(2):
-            water = jnp.full((width, LANES), mask_ref[t + k], jnp.int32) == 1
-            oce[t + k] = jnp.where(water, result[:, k * LANES : (k + 1) * LANES].astype(F32), 0.0).astype(BF16)
-
-    def oce_copy(t, index):
-        return pltpu.make_async_copy(oce.at[pl.ds(t, 4)], oce_hbm.at[pl.ds(t, 4)], oce_sem.at[index])
-
-    for t in range(tiles):
-        regrid(t, t >= tiles - FOLDB)
-
-    for t in range(0, tiles, 2):
-        encode(t)
-        if t % 4 == 2:
-            oce_copy(t - 2, t // 4).start()
-    for t in range(0, tiles, 4):
-        oce_copy(t, t // 4).wait()
+        packed[k // 2, 96 : 96 + fl, (k % 2) * LANES : (k % 2 + 1) * LANES] = (
+            sums[:fl] / sums[fl : fl + 1]
+        ).astype(BF16)
+
+    out = pltpu.make_async_copy(packed, packed_out, packed_sem)
+    out.start()
 
     def leave(c, carry):
         hid_copy(c).wait()
         return carry
 
     lax.fori_loop(0, chunks, leave, 0)
+    out.wait()
+
+
+def finish(
+    mask_ref, hid_in, packed_in, ow_ref, cw_ref, mix_ref,
+    hid_hbm, oce_hbm,
+    packed, wocean, mixt, oce, packed_sem, hid_sem, oce_sem,
+):
+    tiles = oce_hbm.shape[0]
+    och, width = ow_ref.shape
+    fl = cw_ref.shape[0]
+    get = pltpu.make_async_copy(packed_in, packed, packed_sem)
+    get.start()
+    keep = pltpu.make_async_copy(hid_in, hid_hbm, hid_sem)
+    keep.start()
+
+    mixt[...] = mix_ref[...].astype(F32).T.astype(BF16)
+    joined = jnp.concatenate(
+        [
+            ow_ref[...].astype(F32),
+            jnp.zeros((96 - och, width), F32),
+            cw_ref[...].astype(F32),
+            jnp.zeros((LANES - 96 - fl, width), F32),
+        ],
+        axis=0,
+    )
+    wocean[...] = joined.T.astype(BF16)
+    oce[MAXACT] = jnp.zeros((width, LANES), BF16)
+    get.wait()
+    for k in range(0, MAXACT, 2):
+        base = dot(wocean[...], packed[k // 2]).astype(BF16)
+        mixed = dot(mixt[...], base)
+        result = (base.astype(F32) + gelu(mixed)).astype(BF16)
+        oce[k] = result[:, :LANES]
+        oce[k + 1] = result[:, LANES:]
+
+    plain = tiles - FOLDB
+    ahead = tally(mask_ref, plain)
+    copies = []
+    for t in range(tiles):
+        slot = ahead[t] if t < plain else jnp.int32(MAXACT - FOLDB + t - plain)
+        slot = jnp.where(mask_ref[t] == 1, slot, MAXACT)
+        copies.append(pltpu.make_async_copy(oce.at[slot], oce_hbm.at[t], oce_sem.at[t]))
+        copies[-1].start()
+    for copy in copies:
+        copy.wait()
+    keep.wait()
 
 
 def per_device(
@@ -269,20 +312,24 @@
     stride = 3 * channels
     depth = -(-9 * channels // 256) * 256
     rows = (columns - 1) * stride + depth
-    hbm = pl.BlockSpec(memory_space=pl.ANY)
+    hbm = pl.BlockSpec(memory_space=pltpu.HBM)
+    anywhere = pl.BlockSpec(memory_space=pl.ANY)
     vmem = pl.BlockSpec(memory_space=pltpu.VMEM)
     smem = pl.BlockSpec(memory_space=pltpu.SMEM)
     dma = pltpu.SemaphoreType.DMA
-    flops = 2 * columns * lat * width * (12 * channels) + 2 * tiles * cells * width * (width + 128)
-    return pl.pallas_call(
+    hidden, packed = pl.pallas_call(
         functools.partial(kernel, strips),
         out_shape=(
-            jax.ShapeDtypeStruct((columns, width, lat), BF16),
-            jax.ShapeDtypeStruct((tiles, width, cells), BF16),
+            pltpu.VMEM((columns, width, lat), BF16),
+            pltpu.VMEM((MAXACT // 2, LANES, 2 * cells), BF16),
         ),
-        in_specs=[smem, smem, hbm, hbm, vmem, hbm, vmem, vmem, vmem, vmem, hbm],
-        out_specs=(hbm, hbm),
+        in_specs=[hbm] * 8,
+        out_specs=(anywhere, anywhere),
         scratch_shapes=[
+            pltpu.SMEM(pair_tile.shape[::-1], jnp.int32),
+            pltpu.SMEM(ocean_mask.shape, jnp.int32),
+            pltpu.VMEM(lift_weight.shape, BF16),
+            pltpu.VMEM(flux_weight.shape[::-1], BF16),
             pltpu.VMEM((columns + 2, channels, lat), BF16),
             pltpu.VMEM(conv_weight.shape, BF16),
             pltpu.VMEM((och, tiles, cells), BF16),
@@ -292,14 +339,12 @@
             pltpu.VMEM((width, depth), BF16),
             pltpu.VMEM((width, channels), BF16),
             pltpu.VMEM((och * tiles, cells), F32),
-            pltpu.VMEM((width, LANES), BF16),
-            pltpu.VMEM((width, width), BF16),
+            pltpu.VMEM((tiles, LANES, cells), BF16),
+            pltpu.VMEM((MAXACT // 2, LANES, 2 * cells), BF16),
             pltpu.VMEM((3, lat // TLAT, fl, LANES), BF16),
             pltpu.VMEM((fl, LANES), BF16),
             pltpu.VMEM((chunks, columns, width, LANES), BF16),
-            pltpu.VMEM((tiles, LANES, cells), BF16),
-            pltpu.VMEM((tiles, width, cells), BF16),
-            dma((3,)),
+            dma((7,)),
             dma((2,)),
             dma((2,)),
             dma((2,)),
@@ -307,16 +352,40 @@
             dma((chunks, 2)),
             dma((2,)),
             dma((chunks,)),
-            dma((tiles // 4,)),
+            dma,
         ],
         compiler_params=pltpu.CompilerParams(
-            collective_id=0, has_side_effects=True, vmem_limit_bytes=56 * 1024 * 1024
+            collective_id=0, has_side_effects=True, vmem_limit_bytes=61 * 1024 * 1024
         ),
-        cost_estimate=pl.CostEstimate(flops=flops, bytes_accessed=8 * 1024 * 1024, transcendentals=2 * 1024 * 1024),
+        cost_estimate=pl.CostEstimate(
+            flops=24 * columns * lat * width * channels, bytes_accessed=8 * 1024 * 1024, transcendentals=1024 * 1024
+        ),
     )(
         pair_tile.T, ocean_mask, atm_in, ocean_in.transpose(1, 0, 2), lift_weight, conv_weight,
-        flux_weight.T, ocean_weight, couple_weight, mix_weight, regrid_weight,
-    )
+        flux_weight.T, regrid_weight,
+    )
+    return pl.pallas_call(
+        finish,
+        out_shape=(
+            jax.ShapeDtypeStruct((columns, width, lat), BF16),
+            jax.ShapeDtypeStruct((tiles, width, cells), BF16),
+        ),
+        in_specs=[smem, anywhere, anywhere, vmem, vmem, vmem],
+        out_specs=(anywhere, anywhere),
+        scratch_shapes=[
+            pltpu.VMEM((MAXACT // 2, LANES, 2 * cells), BF16),
+            pltpu.VMEM((width, LANES), BF16),
+            pltpu.VMEM((width, width), BF16),
+            pltpu.VMEM((MAXACT + 1, width, cells), BF16),
+            dma,
+            dma,
+            dma((tiles,)),
+        ],
+        compiler_params=pltpu.CompilerParams(vmem_limit_bytes=50 * 1024 * 1024),
+        cost_estimate=pl.CostEstimate(
+            flops=2 * MAXACT * cells * width * (width + 128), bytes_accessed=8 * 1024 * 1024, transcendentals=1024 * 1024
+        ),
+    )(ocean_mask, hidden, packed, ocean_weight, couple_weight, mix_weight)
 
 
 def solution(mesh):

time: 29.4 us -> 24.9 us (0.85)
  local copies, waits for them, and re-layouts: 4.57 us -> 0.02 us
    unnamed x4 -> x8, local copies, waits for them, and re-layouts: 4.57 us -> 0.02 us
    pallas_call x1 -> x2, Pallas kernels: 24 us -> 24 us  [the longest x1 21.5 us: per_device(): pl.pallas_call(functools.partial(kernel, strips), out_shape=(pltpu.VMEM((...]
where the time goes in v2:
time: 24.9 us; the launch traced here: 24.8 us
  Pallas kernels  24 us (96%)
  between operations  0.71 us (3%)
    pallas_call x1, Pallas kernels, per_device(): pl.pallas_call(functools.partial(kernel, strips), out_shape=(pltpu.VMEM((...  21.5 us
    pallas_call x1, Pallas kernels, per_device(): pl.pallas_call(finish, out_shape=(jax.ShapeDtypeStruct((columns, width, l...  2.54 us

profile of v2, /device:TPU:0, one launch (start us, length us, event | category | flops | bytes accessed | tf_op | source)
XLA Modules:
  0.0 24.8 jit_solution(7365019443188920700)
XLA Ops:
  0.6 0.0 copy-start
  0.6 0.0 copy-start.1
  0.7 0.0 copy-start.2
  0.7 0.0 copy-start.3
  0.7 21.5 %shard_map.122 = (bf16[8,256,640]{2,1,0:T(8,128)(2,1)S(1)}, bf16[4,128,256]{2,1,0:T(8,128)(2,1)S(1)}) custom-call(s32[3,16]{1,0:T(4,128)} %bitcast.5, s32[16]{0:T(128)} %mask_ref.1, bf16[8,48,640]{2,1,0:T(8,128)(2,1)} %atm_hbm.1, bf16[95,16,128]{2,1,0:T(8,128)(2,1)} %bitcast.3, bf16[48,256]{1,0:T(8,128)(2,1)} %lift_hbm.1, bf16[3,3,256,256]{3,2,1,0:T(8,128)(2,1)} %conv_hbm.1, ...), custom_call_target="tpu_custom_call" | custom-call | flops 1509949440 | bytes 8388608 | tf_op jit(solution)/shard_map/pallas_call | solution.py:320
  22.2 0.0 copy-done
  22.2 0.0 copy-done.1
  22.2 0.0 copy-done.2
  22.2 0.0 copy-done.3
  22.2 2.5 %shard_map.123 = (bf16[8,256,640]{2,1,0:T(8,128)(2,1)}, bf16[16,256,128]{2,1,0:T(8,128)(2,1)}) custom-call(s32[16]{0:T(128)S(1)} %copy-done.3, bf16[8,256,640]{2,1,0:T(8,128)(2,1)S(1)} %get-tuple-element.4.hid_in, bf16[4,128,256]{2,1,0:T(8,128)(2,1)S(1)} %get-tuple-element.5.packed_in, bf16[95,256]{1,0:T(8,128)(2,1)S(1)} %copy-done.1, ...), custom_call_target="tpu_custom_call" | custom-call | flops 201326592 | bytes 8388608 | tf_op jit(solution)/shard_map/pallas_call | solution.py:367
Async XLA Ops:
  0.6 21.6 %copy-start = (bf16[256,256]{1,0:T(8,128)(2,1)S(1)}, bf16[256,256]{1,0:T(8,128)(2,1)}, u32[]{:S(2)}) copy-start(bf16[256,256]{1,0:T(8,128)(2,1)} %mix_ref.1) | copy-start | bytes 393220
  0.6 21.6 %copy-start.1 = (bf16[95,256]{1,0:T(8,128)(2,1)S(1)}, bf16[95,256]{1,0:T(8,128)(2,1)}, u32[]{:S(2)}) copy-start(bf16[95,256]{1,0:T(8,128)(2,1)} %ow_ref.1) | copy-start | bytes 145924
  0.7 21.6 %copy-start.2 = (bf16[16,256]{1,0:T(8,128)(2,1)S(1)}, bf16[16,256]{1,0:T(8,128)(2,1)}, u32[]{:S(2)}) copy-start(bf16[16,256]{1,0:T(8,128)(2,1)} %cw_ref.1) | copy-start | bytes 24580
  0.7 21.6 %copy-start.3 = (s32[16]{0:T(128)S(1)}, s32[16]{0:T(128)}, u32[]{:S(2)}) copy-start(s32[16]{0:T(128)} %mask_ref.1) | copy-start | bytes 196

commit v3 on v2

--- a/solution.py
+++ b/solution.py
@@ -16,8 +16,8 @@
 BF16 = jnp.bfloat16
 
 
-def gelu(z):
-    return 0.5 * z * (1.0 + jnp.tanh(0.7978845608028654 * (z + 0.044715 * z * z * z)))
+def half_gelu(h):
+    return h * jnp.tanh(h * (1.5957691216057308 + 0.285419265090401 * (h * h)))
 
 
 def dot(a, b):
@@ -41,19 +41,24 @@
     return blocks
 
 
-def tally(mask, count):
-    ahead = [jnp.int32(0)]
-    for t in range(count - 1):
-        ahead.append(ahead[-1] + mask[t])
-    return ahead
+def water_slots(mask, tiles):
+    plain = tiles - FOLDB
+    slots = [jnp.int32(0)] * (MAXACT - FOLDB)
+    count = jnp.int32(0)
+    for t in range(plain):
+        wet = mask[t] == 1
+        for k in range(min(t + 1, MAXACT - FOLDB)):
+            slots[k] = jnp.where(wet & (count == k), t, slots[k])
+        count = count + mask[t]
+    return slots + [plain + k for k in range(FOLDB)], count
 
 
 def kernel(
     strips,
     pair_hbm, mask_hbm, atm_hbm, ocean_hbm, lift_hbm, conv_hbm, flux_hbm, regrid_hbm,
     hid_out, packed_out,
-    pair_ref, mask_ref, lift_ref, flux_ref, xin, conv_v, ocean_v, regrid_v, col, folded_f, wt, lt, ocean_f, ustate, packed, table, mirror, hid,
-    load_sem, regrid_sem, halo_send, halo_recv, flux_send, flux_recv, mir_sem, hid_sem, packed_sem,
+    pair_ref, mask_ref, lift_ref, flux_ref, xin, conv_v, ocean_v, regrid_v, col, folded_f, wt, lt, ocean_f, ustate, table, mirror,
+    load_sem, regrid_sem, halo_send, halo_recv, flux_send, flux_recv, mir_sem,
 ):
     columns, channels, lat = atm_hbm.shape
     width = lift_ref.shape[1]
@@ -136,7 +141,7 @@
         folded_f[k * channels : (k + 1) * channels, :] = dot(lift_ref[...], conv_v[k // 3, k % 3])
         if k < columns:
             spread(k + 1)
-    wt[...] = folded_f[...].T.astype(BF16)
+    wt[...] = (0.5 * folded_f[...]).T.astype(BF16)
 
     halo_r.wait()
     halo_l.wait()
@@ -149,45 +154,43 @@
             table.at[1, rows], table.at[side, rows], flux_send.at[c, index], flux_recv.at[c, index], to
         )
 
-    def hid_copy(c):
-        return pltpu.make_async_copy(
-            hid.at[c], hid_out.at[:, :, pl.ds(pl.multiple_of(c * LANES, LANES), LANES)], hid_sem.at[c]
+    to_fold = remote(table.at[1, chunks * per - 1], mirror, mir_sem.at[0], mir_sem.at[1], fold)
+
+    def convolve(c, x):
+        rhs = jnp.concatenate(
+            [col[c, x * stride : x * stride + depth, :], col[c, (x + 1) * stride : (x + 1) * stride + depth, :]],
+            axis=1,
         )
-
-    to_fold = remote(table.at[1, chunks * per - 1], mirror, mir_sem.at[0], mir_sem.at[1], fold)
-
-    def chunk(i, carry):
-        c = chunks - 1 - i
-        flux = []
-        for x in range(0, columns, 2):
-            rhs = jnp.concatenate(
-                [col[c, x * stride : x * stride + depth, :], col[c, (x + 1) * stride : (x + 1) * stride + depth, :]],
-                axis=1,
-            )
-            at = (x + 1) * stride + channels
-            mid = jnp.concatenate(
-                [col[c, at : at + channels, :], col[c, at + stride : at + stride + channels, :]], axis=1
-            )
-            conv = dot(wt[...], rhs)
-            lifted = dot(lt[...], mid).astype(BF16).astype(F32)
-            hidden = (lifted + gelu(conv)).astype(BF16)
-            hid[c, x] = hidden[:, :LANES]
-            hid[c, x + 1] = hidden[:, LANES:]
-            f = dot(flux_ref[...], hidden)
-            flux += [f[:, :LANES], f[:, LANES:]]
-        hid_copy(c).start()
+        at = (x + 1) * stride + channels
+        mid = jnp.concatenate([col[c, at : at + channels, :], col[c, at + stride : at + stride + channels, :]], axis=1)
+        return dot(wt[...], rhs), dot(lt[...], mid)
+
+    def activate(c, x, half, lifted):
+        hidden = (lifted + half + half_gelu(half)).astype(BF16)
+        hid_out[x, :, c * LANES : (c + 1) * LANES] = hidden[:, :LANES]
+        hid_out[x + 1, :, c * LANES : (c + 1) * LANES] = hidden[:, LANES:]
+        f = dot(flux_ref[...], hidden)
+        return [f[:, :LANES], f[:, LANES:]]
+
+    def send(c, flux):
         for a, tile in enumerate(regroup(flux, TLAT)):
             table[1, c * per + a] = tile.astype(BF16)
         flux_copy(c, right, 0, 0).start()
         flux_copy(c, left, 2, 1).start()
-
-        @pl.when(i == 0)
-        def _():
+        if c == chunks - 1:
             to_fold.start()
 
-        return carry
-
-    lax.fori_loop(0, chunks, chunk, 0)
+    work = [(c, x) for c in reversed(range(chunks)) for x in range(0, columns, 2)]
+    flux = []
+    ready = convolve(*work[0])
+    for i, (c, x) in enumerate(work):
+        now = ready
+        if i + 1 < len(work):
+            ready = convolve(*work[i + 1])
+        flux += activate(c, x, *now)
+        if len(flux) == columns:
+            send(c, flux)
+            flux = []
 
     load_ocean.wait()
     ocean_f[...] = ocean_v[...].astype(F32).reshape(ocean_f.shape)
@@ -195,17 +198,9 @@
         ustate[t, 80:, :] = jnp.zeros((ustate.shape[1] - 80, LANES), BF16)
         ustate[t, 0:och, :] = ocean_f[pl.ds(t, och, stride=tiles), :].astype(BF16)
 
-    plain = tiles - FOLDB
-    ahead = tally(mask_ref, plain)
-    slots = []
-    for k in range(MAXACT - FOLDB):
-        slot = jnp.int32(0)
-        for t in range(k, plain):
-            slot = jnp.where((mask_ref[t] == 1) & (ahead[t] == k), t, slot)
-        slots.append(slot)
-    slots += [plain + k for k in range(FOLDB)]
+    slots, _ = water_slots(mask_ref, tiles)
     for k, t in enumerate(slots):
-        packed[k // 2, :, (k % 2) * LANES : (k % 2 + 1) * LANES] = ustate[t]
+        packed_out[k // 2, :, (k % 2) * LANES : (k % 2 + 1) * LANES] = ustate[t]
 
     load_main.wait()
     load_fold.wait()
@@ -229,33 +224,36 @@
         lhs = jnp.concatenate([jnp.concatenate([g, ones], axis=0) for g in got], axis=1)
         rhs = jnp.concatenate(weights, axis=1)
         sums = lax.dot_general(lhs, rhs, (((1,), (1,)), ((), ())), preferred_element_type=F32)
-        packed[k // 2, 96 : 96 + fl, (k % 2) * LANES : (k % 2 + 1) * LANES] = (
+        packed_out[k // 2, 96 : 96 + fl, (k % 2) * LANES : (k % 2 + 1) * LANES] = (
             sums[:fl] / sums[fl : fl + 1]
         ).astype(BF16)
 
-    out = pltpu.make_async_copy(packed, packed_out, packed_sem)
-    out.start()
-
-    def leave(c, carry):
-        hid_copy(c).wait()
-        return carry
-
-    lax.fori_loop(0, chunks, leave, 0)
-    out.wait()
-
 
 def finish(
-    mask_ref, hid_in, packed_in, ow_ref, cw_ref, mix_ref,
+    mask_ref, hid_in, packed, ow_ref, cw_ref, mix_ref,
     hid_hbm, oce_hbm,
-    packed, wocean, mixt, oce, packed_sem, hid_sem, oce_sem,
+    wocean, mixt, oce, hid_sem, land_sem, water_sem,
 ):
     tiles = oce_hbm.shape[0]
     och, width = ow_ref.shape
     fl = cw_ref.shape[0]
-    get = pltpu.make_async_copy(packed_in, packed, packed_sem)
-    get.start()
     keep = pltpu.make_async_copy(hid_in, hid_hbm, hid_sem)
     keep.start()
+
+    plain = tiles - FOLDB
+    oce[MAXACT] = jnp.zeros((width, LANES), BF16)
+    land = [pltpu.make_async_copy(oce.at[MAXACT], oce_hbm.at[t], land_sem.at[t]) for t in range(plain)]
+    for t in range(plain):
+        pl.when(mask_ref[t] == 0)(land[t].start)
+
+    slots, count = water_slots(mask_ref, tiles)
+    water = [pltpu.make_async_copy(oce.at[k], oce_hbm.at[t], water_sem.at[k]) for k, t in enumerate(slots)]
+
+    def if_water(k, act):
+        if k < MAXACT - FOLDB:
+            pl.when(k < count)(act)
+        else:
+            act()
 
     mixt[...] = mix_ref[...].astype(F32).T.astype(BF16)
     joined = jnp.concatenate(
@@ -268,25 +266,20 @@
         axis=0,
     )
     wocean[...] = joined.T.astype(BF16)
-    oce[MAXACT] = jnp.zeros((width, LANES), BF16)
-    get.wait()
-    for k in range(0, MAXACT, 2):
-        base = dot(wocean[...], packed[k // 2]).astype(BF16)
-        mixed = dot(mixt[...], base)
-        result = (base.astype(F32) + gelu(mixed)).astype(BF16)
-        oce[k] = result[:, :LANES]
-        oce[k + 1] = result[:, LANES:]
-
-    plain = tiles - FOLDB
-    ahead = tally(mask_ref, plain)
-    copies = []
-    for t in range(tiles):
-        slot = ahead[t] if t < plain else jnp.int32(MAXACT - FOLDB + t - plain)
-        slot = jnp.where(mask_ref[t] == 1, slot, MAXACT)
-        copies.append(pltpu.make_async_copy(oce.at[slot], oce_hbm.at[t], oce_sem.at[t]))
-        copies[-1].start()
-    for copy in copies:
-        copy.wait()
+    for first in range(0, MAXACT, 4):
+        for k in range(first, first + 4, 2):
+            base = dot(wocean[...], packed[k // 2]).astype(BF16)
+            half = 0.5 * dot(mixt[...], base)
+            result = (base.astype(F32) + half + half_gelu(half)).astype(BF16)
+            oce[k] = result[:, :LANES]
+            oce[k + 1] = result[:, LANES:]
+        for k in range(first, first + 4):
+            if_water(k, water[k].start)
+
+    for k in range(MAXACT):
+        if_water(k, water[k].wait)
+    for t in range(plain):
+        pl.when(mask_ref[t] == 0)(land[t].wait)
     keep.wait()
 
 
@@ -324,7 +317,7 @@
             pltpu.VMEM((MAXACT // 2, LANES, 2 * cells), BF16),
         ),
         in_specs=[hbm] * 8,
-        out_specs=(anywhere, anywhere),
+        out_specs=(vmem, vmem),
         scratch_shapes=[
             pltpu.SMEM(pair_tile.shape[::-1], jnp.int32),
             pltpu.SMEM(ocean_mask.shape, jnp.int32),
@@ -340,10 +333,8 @@
             pltpu.VMEM((width, channels), BF16),
             pltpu.VMEM((och * tiles, cells), F32),
             pltpu.VMEM((tiles, LANES, cells), BF16),
-            pltpu.VMEM((MAXACT // 2, LANES, 2 * cells), BF16),
             pltpu.VMEM((3, lat // TLAT, fl, LANES), BF16),
             pltpu.VMEM((fl, LANES), BF16),
-            pltpu.VMEM((chunks, columns, width, LANES), BF16),
             dma((7,)),
             dma((2,)),
             dma((2,)),
@@ -351,8 +342,6 @@
             dma((chunks, 2)),
             dma((chunks, 2)),
             dma((2,)),
-            dma((chunks,)),
-            dma,
         ],
         compiler_params=pltpu.CompilerParams(
             collective_id=0, has_side_effects=True, vmem_limit_bytes=61 * 1024 * 1024
@@ -370,16 +359,15 @@
             jax.ShapeDtypeStruct((columns, width, lat), BF16),
             jax.ShapeDtypeStruct((tiles, width, cells), BF16),
         ),
-        in_specs=[smem, anywhere, anywhere, vmem, vmem, vmem],
+        in_specs=[smem, anywhere, vmem, vmem, vmem, vmem],
         out_specs=(anywhere, anywhere),
         scratch_shapes=[
-            pltpu.VMEM((MAXACT // 2, LANES, 2 * cells), BF16),
             pltpu.VMEM((width, LANES), BF16),
             pltpu.VMEM((width, width), BF16),
             pltpu.VMEM((MAXACT + 1, width, cells), BF16),
             dma,
-            dma,
             dma((tiles,)),
+            dma((MAXACT,)),
         ],
         compiler_params=pltpu.CompilerParams(vmem_limit_bytes=50 * 1024 * 1024),
         cost_estimate=pl.CostEstimate(

time: 24.9 us -> 23.9 us (0.960)
  Pallas kernels: 24 us -> 23 us
    pallas_call x1, Pallas kernels: 21.5 us -> 20.1 us  [per_device(): pl.pallas_call(functools.partial(kernel, strips), out_shape=(pltpu.VMEM((...]
    pallas_call x1, Pallas kernels: 2.54 us -> 2.96 us  [per_device(): pl.pallas_call(finish, out_shape=(jax.ShapeDtypeStruct((columns, width, l...]
where the time goes in v3:
time: 23.9 us; the launch traced here: 23.7 us
  Pallas kernels  23 us (96%)
  between operations  0.71 us (3%)
    pallas_call x1, Pallas kernels, per_device(): pl.pallas_call(functools.partial(kernel, strips), out_shape=(pltpu.VMEM((...  20.1 us
    pallas_call x1, Pallas kernels, per_device(): pl.pallas_call(finish, out_shape=(jax.ShapeDtypeStruct((columns, width, l...  2.96 us

profile of v3, /device:TPU:0, one launch (start us, length us, event | category | flops | bytes accessed | tf_op | source)
XLA Modules:
  0.0 23.7 jit_solution(5033443785415219045)
XLA Ops:
  0.6 0.0 copy-start
  0.6 0.0 copy-start.1
  0.7 0.0 copy-start.2
  0.7 0.0 copy-start.3
  0.7 20.1 %shard_map.122 = (bf16[8,256,640]{2,1,0:T(8,128)(2,1)S(1)}, bf16[4,128,256]{2,1,0:T(8,128)(2,1)S(1)}) custom-call(s32[3,16]{1,0:T(4,128)} %bitcast.5, s32[16]{0:T(128)} %mask_ref.1, bf16[8,48,640]{2,1,0:T(8,128)(2,1)} %atm_hbm.1, bf16[95,16,128]{2,1,0:T(8,128)(2,1)} %bitcast.3, bf16[48,256]{1,0:T(8,128)(2,1)} %lift_hbm.1, bf16[3,3,256,256]{3,2,1,0:T(8,128)(2,1)} %conv_hbm.1, ...), custom_call_target="tpu_custom_call" | custom-call | flops 1509949440 | bytes 8388608 | tf_op jit(solution)/shard_map/pallas_call | solution.py:313
  20.7 0.0 copy-done
  20.7 0.0 copy-done.1
  20.8 0.0 copy-done.2
  20.8 0.0 copy-done.3
  20.8 3.0 %shard_map.123 = (bf16[8,256,640]{2,1,0:T(8,128)(2,1)}, bf16[16,256,128]{2,1,0:T(8,128)(2,1)}) custom-call(s32[16]{0:T(128)S(1)} %copy-done.3, bf16[8,256,640]{2,1,0:T(8,128)(2,1)S(1)} %get-tuple-element.4.hid_in, bf16[4,128,256]{2,1,0:T(8,128)(2,1)S(1)} %get-tuple-element.5.packed, bf16[95,256]{1,0:T(8,128)(2,1)S(1)} %copy-done.1, ...), custom_call_target="tpu_custom_call" | custom-call | flops 201326592 | bytes 8388608 | tf_op jit(solution)/shard_map/pallas_call | solution.py:356
Async XLA Ops:
  0.6 20.1 %copy-start = (bf16[256,256]{1,0:T(8,128)(2,1)S(1)}, bf16[256,256]{1,0:T(8,128)(2,1)}, u32[]{:S(2)}) copy-start(bf16[256,256]{1,0:T(8,128)(2,1)} %mix_ref.1) | copy-start | bytes 393220
  0.6 20.1 %copy-start.1 = (bf16[95,256]{1,0:T(8,128)(2,1)S(1)}, bf16[95,256]{1,0:T(8,128)(2,1)}, u32[]{:S(2)}) copy-start(bf16[95,256]{1,0:T(8,128)(2,1)} %ow_ref.1) | copy-start | bytes 145924
  0.7 20.1 %copy-start.2 = (bf16[16,256]{1,0:T(8,128)(2,1)S(1)}, bf16[16,256]{1,0:T(8,128)(2,1)}, u32[]{:S(2)}) copy-start(bf16[16,256]{1,0:T(8,128)(2,1)} %cw_ref.1) | copy-start | bytes 24580
  0.7 20.1 %copy-start.3 = (s32[16]{0:T(128)S(1)}, s32[16]{0:T(128)}, u32[]{:S(2)}) copy-start(s32[16]{0:T(128)} %mask_ref.1) | copy-start | bytes 196

commit v4 on v3

--- a/solution.py
+++ b/solution.py
@@ -50,14 +50,14 @@
         for k in range(min(t + 1, MAXACT - FOLDB)):
             slots[k] = jnp.where(wet & (count == k), t, slots[k])
         count = count + mask[t]
-    return slots + [plain + k for k in range(FOLDB)], count
+    return slots + [plain + k for k in range(FOLDB)]
 
 
 def kernel(
     strips,
-    pair_hbm, mask_hbm, atm_hbm, ocean_hbm, lift_hbm, conv_hbm, flux_hbm, regrid_hbm,
-    hid_out, packed_out,
-    pair_ref, mask_ref, lift_ref, flux_ref, xin, conv_v, ocean_v, regrid_v, col, folded_f, wt, lt, ocean_f, ustate, table, mirror,
+    pair_hbm, mask_hbm, atm_hbm, ocean_hbm, lift_hbm, conv_hbm, flux_hbm, ow_hbm, cw_hbm, mix_hbm, regrid_hbm,
+    hid_out, packed_out, wocean_out, mixt_out, from_hbm,
+    pair_ref, mask_ref, from_ref, lift_ref, flux_ref, ow_ref, cw_ref, mix_ref, xin, conv_v, ocean_v, regrid_v, col, folded_f, wt, lt, ocean_f, ustate, mine, sides, mirror, partial,
     load_sem, regrid_sem, halo_send, halo_recv, flux_send, flux_recv, mir_sem,
 ):
     columns, channels, lat = atm_hbm.shape
@@ -94,6 +94,10 @@
         regrid_v.at[pl.ds(tiles - FOLDB, FOLDB), pl.ds(3, 1)],
         regrid_sem.at[1],
     )
+    load_ows = [
+        pltpu.make_async_copy(source, target, load_sem.at[7 + i])
+        for i, (source, target) in enumerate(((ow_hbm, ow_ref), (cw_hbm, cw_ref), (mix_hbm, mix_ref)))
+    ]
     smalls = [
         pltpu.make_async_copy(source, target, load_sem.at[3 + i])
         for i, (source, target) in enumerate(
@@ -133,6 +137,8 @@
     load_atm.wait()
     load_conv.wait()
     load_ocean.start()
+    for load in load_ows:
+        load.start()
     load_main.start()
     load_fold.start()
     for small in smalls[1:]:
@@ -143,18 +149,13 @@
             spread(k + 1)
     wt[...] = (0.5 * folded_f[...]).T.astype(BF16)
 
-    halo_r.wait()
-    halo_l.wait()
-    spread(0)
-    spread(columns + 1)
-
-    def flux_copy(c, to, side, index):
+    def flux_copy(c, to, side):
         rows = pl.ds(c * per, per)
         return remote(
-            table.at[1, rows], table.at[side, rows], flux_send.at[c, index], flux_recv.at[c, index], to
+            mine.at[rows], sides.at[side, rows], flux_send.at[c, side], flux_recv.at[c, side], to
         )
 
-    to_fold = remote(table.at[1, chunks * per - 1], mirror, mir_sem.at[0], mir_sem.at[1], fold)
+    to_fold = remote(mine.at[chunks * per - 1], mirror, mir_sem.at[0], mir_sem.at[1], fold)
 
     def convolve(c, x):
         rhs = jnp.concatenate(
@@ -174,23 +175,31 @@
 
     def send(c, flux):
         for a, tile in enumerate(regroup(flux, TLAT)):
-            table[1, c * per + a] = tile.astype(BF16)
-        flux_copy(c, right, 0, 0).start()
-        flux_copy(c, left, 2, 1).start()
+            mine[c * per + a] = tile.astype(BF16)
+        flux_copy(c, right, 0).start()
+        flux_copy(c, left, 1).start()
         if c == chunks - 1:
             to_fold.start()
 
-    work = [(c, x) for c in reversed(range(chunks)) for x in range(0, columns, 2)]
-    flux = []
-    ready = convolve(*work[0])
-    for i, (c, x) in enumerate(work):
-        now = ready
-        if i + 1 < len(work):
-            ready = convolve(*work[i + 1])
-        flux += activate(c, x, *now)
-        if len(flux) == columns:
-            send(c, flux)
-            flux = []
+    def sweep(work):
+        ready = convolve(*work[0])
+        for i, (c, x) in enumerate(work):
+            now = ready
+            if i + 1 < len(work):
+                ready = convolve(*work[i + 1])
+            flux[c, x], flux[c, x + 1] = activate(c, x, *now)
+            if x + 2 == columns:
+                send(c, [flux.pop((c, k)) for k in range(columns)])
+
+    flux = {}
+    bands = list(reversed(range(chunks)))
+    sweep([(c, x) for c in bands for x in range(2, columns - 2, 2)])
+    halo_r.wait()
+    halo_l.wait()
+    spread(0)
+    spread(columns + 1)
+
+    sweep([(c, x) for c in bands for x in (0, columns - 2)])
 
     load_ocean.wait()
     ocean_f[...] = ocean_v[...].astype(F32).reshape(ocean_f.shape)
@@ -198,64 +207,20 @@
         ustate[t, 80:, :] = jnp.zeros((ustate.shape[1] - 80, LANES), BF16)
         ustate[t, 0:och, :] = ocean_f[pl.ds(t, och, stride=tiles), :].astype(BF16)
 
-    slots, _ = water_slots(mask_ref, tiles)
+    slots = water_slots(mask_ref, tiles)
+    ahead = jnp.int32(0)
+    for t in range(tiles):
+        slot = ahead if t < tiles - FOLDB else jnp.int32(MAXACT - tiles + t)
+        from_ref[t] = jnp.where(mask_ref[t] == 1, slot, MAXACT)
+        ahead = ahead + mask_ref[t]
+    give_from = pltpu.make_async_copy(from_ref, from_hbm, load_sem.at[10])
+    give_from.start()
     for k, t in enumerate(slots):
         packed_out[k // 2, :, (k % 2) * LANES : (k % 2 + 1) * LANES] = ustate[t]
 
-    load_main.wait()
-    load_fold.wait()
-
-    def arrive(c, carry):
-        flux_copy(c, right, 0, 0).wait()
-        flux_copy(c, left, 2, 1).wait()
-        return carry
-
-    lax.fori_loop(0, chunks, arrive, 0)
-    to_fold.wait()
-
-    ones = jnp.ones((fl, LANES), BF16)
-    mirrored = mirror[...]
-    for k, t in enumerate(slots):
-        got = [table[p, pair_ref[p, t]] for p in range(3)]
-        weights = [regrid_v[t, p] for p in range(3)]
-        if k >= MAXACT - FOLDB:
-            got.append(mirrored)
-            weights.append(regrid_v[t, 3])
-        lhs = jnp.concatenate([jnp.concatenate([g, ones], axis=0) for g in got], axis=1)
-        rhs = jnp.concatenate(weights, axis=1)
-        sums = lax.dot_general(lhs, rhs, (((1,), (1,)), ((), ())), preferred_element_type=F32)
-        packed_out[k // 2, 96 : 96 + fl, (k % 2) * LANES : (k % 2 + 1) * LANES] = (
-            sums[:fl] / sums[fl : fl + 1]
-        ).astype(BF16)
-
-
-def finish(
-    mask_ref, hid_in, packed, ow_ref, cw_ref, mix_ref,
-    hid_hbm, oce_hbm,
-    wocean, mixt, oce, hid_sem, land_sem, water_sem,
-):
-    tiles = oce_hbm.shape[0]
-    och, width = ow_ref.shape
-    fl = cw_ref.shape[0]
-    keep = pltpu.make_async_copy(hid_in, hid_hbm, hid_sem)
-    keep.start()
-
-    plain = tiles - FOLDB
-    oce[MAXACT] = jnp.zeros((width, LANES), BF16)
-    land = [pltpu.make_async_copy(oce.at[MAXACT], oce_hbm.at[t], land_sem.at[t]) for t in range(plain)]
-    for t in range(plain):
-        pl.when(mask_ref[t] == 0)(land[t].start)
-
-    slots, count = water_slots(mask_ref, tiles)
-    water = [pltpu.make_async_copy(oce.at[k], oce_hbm.at[t], water_sem.at[k]) for k, t in enumerate(slots)]
-
-    def if_water(k, act):
-        if k < MAXACT - FOLDB:
-            pl.when(k < count)(act)
-        else:
-            act()
-
-    mixt[...] = mix_ref[...].astype(F32).T.astype(BF16)
+    for load in load_ows:
+        load.wait()
+    mixt_out[...] = (0.5 * mix_ref[...].astype(F32)).T.astype(BF16)
     joined = jnp.concatenate(
         [
             ow_ref[...].astype(F32),
@@ -265,21 +230,63 @@
         ],
         axis=0,
     )
-    wocean[...] = joined.T.astype(BF16)
-    for first in range(0, MAXACT, 4):
-        for k in range(first, first + 4, 2):
-            base = dot(wocean[...], packed[k // 2]).astype(BF16)
-            half = 0.5 * dot(mixt[...], base)
-            result = (base.astype(F32) + half + half_gelu(half)).astype(BF16)
-            oce[k] = result[:, :LANES]
-            oce[k + 1] = result[:, LANES:]
-        for k in range(first, first + 4):
-            if_water(k, water[k].start)
-
-    for k in range(MAXACT):
-        if_water(k, water[k].wait)
-    for t in range(plain):
-        pl.when(mask_ref[t] == 0)(land[t].wait)
+    wocean_out[...] = joined.T.astype(BF16)
+
+    load_main.wait()
+    load_fold.wait()
+    ones = jnp.ones((fl, LANES), BF16)
+
+    def weigh(t, blocks, got):
+        lhs = jnp.concatenate([jnp.concatenate([g, ones], axis=0) for g in got], axis=1)
+        rhs = jnp.concatenate([regrid_v[t, p] for p in blocks], axis=1)
+        return lax.dot_general(lhs, rhs, (((1,), (1,)), ((), ())), preferred_element_type=F32)
+
+    for k, t in enumerate(slots):
+        partial[k] = weigh(t, (1,), [mine[pair_ref[1, t]]])
+
+    def arrive(c, carry):
+        flux_copy(c, right, 0).wait()
+        flux_copy(c, left, 1).wait()
+        return carry
+
+    lax.fori_loop(0, chunks, arrive, 0)
+    to_fold.wait()
+    give_from.wait()
+
+    for k, t in enumerate(slots):
+        blocks, got = (0, 2), [sides[p // 2, pair_ref[p, t]] for p in (0, 2)]
+        if k >= MAXACT - FOLDB:
+            blocks, got = blocks + (3,), got + [mirror[...]]
+        sums = partial[k] + weigh(t, blocks, got)
+        packed_out[k // 2, 96 : 96 + fl, (k % 2) * LANES : (k % 2 + 1) * LANES] = (
+            sums[:fl] / sums[fl : fl + 1]
+        ).astype(BF16)
+
+
+def finish(
+    from_hbm, hid_in, packed, wocean, mixt,
+    hid_hbm, oce_hbm,
+    from_ref, oce, from_sem, hid_sem, oce_sem,
+):
+    tiles, width = oce_hbm.shape[:2]
+    get_from = pltpu.make_async_copy(from_hbm, from_ref, from_sem)
+    get_from.start()
+    keep = pltpu.make_async_copy(hid_in, hid_hbm, hid_sem)
+    keep.start()
+    oce[MAXACT] = jnp.zeros((width, LANES), BF16)
+    for k in range(0, MAXACT, 2):
+        base = dot(wocean[...], packed[k // 2]).astype(BF16)
+        half = dot(mixt[...], base)
+        result = (base.astype(F32) + half + half_gelu(half)).astype(BF16)
+        oce[k] = result[:, :LANES]
+        oce[k + 1] = result[:, LANES:]
+
+    get_from.wait()
+    copies = [pltpu.make_async_copy(oce.at[from_ref[t]], oce_hbm.at[t], oce_sem.at[t]) for t in range(tiles)]
+    for copy in copies:
+        copy.start()
+    for copy in copies:
+        copy.wait()
     keep.wait()
 
 
@@ -308,21 +315,27 @@
     hbm = pl.BlockSpec(memory_space=pltpu.HBM)
     anywhere = pl.BlockSpec(memory_space=pl.ANY)
     vmem = pl.BlockSpec(memory_space=pltpu.VMEM)
-    smem = pl.BlockSpec(memory_space=pltpu.SMEM)
     dma = pltpu.SemaphoreType.DMA
-    hidden, packed = pl.pallas_call(
+    hidden, *operands, source = pl.pallas_call(
         functools.partial(kernel, strips),
         out_shape=(
             pltpu.VMEM((columns, width, lat), BF16),
             pltpu.VMEM((MAXACT // 2, LANES, 2 * cells), BF16),
+            pltpu.VMEM((width, LANES), BF16),
+            pltpu.VMEM((width, width), BF16),
+            jax.ShapeDtypeStruct((tiles,), jnp.int32),
         ),
-        in_specs=[hbm] * 8,
-        out_specs=(vmem, vmem),
+        in_specs=[hbm] * 11,
+        out_specs=(vmem,) * 4 + (anywhere,),
         scratch_shapes=[
             pltpu.SMEM(pair_tile.shape[::-1], jnp.int32),
             pltpu.SMEM(ocean_mask.shape, jnp.int32),
+            pltpu.SMEM(ocean_mask.shape, jnp.int32),
             pltpu.VMEM(lift_weight.shape, BF16),
             pltpu.VMEM(flux_weight.shape[::-1], BF16),
+            pltpu.VMEM(ocean_weight.shape, BF16),
+            pltpu.VMEM(couple_weight.shape, BF16),
+            pltpu.VMEM(mix_weight.shape, BF16),
             pltpu.VMEM((columns + 2, channels, lat), BF16),
             pltpu.VMEM(conv_weight.shape, BF16),
             pltpu.VMEM((och, tiles, cells), BF16),
@@ -333,9 +346,11 @@
             pltpu.VMEM((width, channels), BF16),
             pltpu.VMEM((och * tiles, cells), F32),
             pltpu.VMEM((tiles, LANES, cells), BF16),
-            pltpu.VMEM((3, lat // TLAT, fl, LANES), BF16),
+            pltpu.VMEM((lat // TLAT, fl, LANES), BF16),
+            pltpu.VMEM((2, lat // TLAT, fl, LANES), BF16),
             pltpu.VMEM((fl, LANES), BF16),
-            dma((7,)),
+            pltpu.VMEM((MAXACT, 2 * fl, LANES), F32),
+            dma((11,)),
             dma((2,)),
             dma((2,)),
             dma((2,)),
@@ -351,7 +366,7 @@
         ),
     )(
         pair_tile.T, ocean_mask, atm_in, ocean_in.transpose(1, 0, 2), lift_weight, conv_weight,
-        flux_weight.T, regrid_weight,
+        flux_weight.T, ocean_weight, couple_weight, mix_weight, regrid_weight,
     )
     return pl.pallas_call(
         finish,
@@ -359,21 +374,20 @@
             jax.ShapeDtypeStruct((columns, width, lat), BF16),
             jax.ShapeDtypeStruct((tiles, width, cells), BF16),
         ),
-        in_specs=[smem, anywhere, vmem, vmem, vmem, vmem],
+        in_specs=[anywhere, anywhere, vmem, vmem, vmem],
         out_specs=(anywhere, anywhere),
         scratch_shapes=[
-            pltpu.VMEM((width, LANES), BF16),
-            pltpu.VMEM((width, width), BF16),
+            pltpu.SMEM((tiles,), jnp.int32),
             pltpu.VMEM((MAXACT + 1, width, cells), BF16),
             dma,
+            dma,
             dma((tiles,)),
-            dma((MAXACT,)),
         ],
-        compiler_params=pltpu.CompilerParams(vmem_limit_bytes=50 * 1024 * 1024),
+        compiler_params=pltpu.CompilerParams(vmem_limit_bytes=61 * 1024 * 1024),
         cost_estimate=pl.CostEstimate(
             flops=2 * MAXACT * cells * width * (width + 128), bytes_accessed=8 * 1024 * 1024, transcendentals=1024 * 1024
         ),
-    )(ocean_mask, hidden, packed, ocean_weight, couple_weight, mix_weight)
+    )(source, hidden, *operands)
 
 
 def solution(mesh):

time: 23.9 us -> 104 us (4.35)
  Pallas kernels: 23 us -> 99.9 us
  local copies, waits for them, and re-layouts: 0.02 us -> 3.47 us
    pallas_call x1, Pallas kernels: 2.96 us -> 81.7 us  [per_device(): pl.pallas_call(finish, out_shape=(jax.ShapeDtypeStruct((columns, width, l...]
    unnamed x8, local copies, waits for them, and re-layouts: 0.02 us -> 3.47 us
    pallas_call x1, Pallas kernels: 20.1 us -> 18.2 us  [per_device(): pl.pallas_call(functools.partial(kernel, strips), out_shape=(pltpu.VMEM((...]
where the time goes in v4:
time: 104 us
  Pallas kernels  99.9 us (96%)
  local copies, waits for them, and re-layouts  3.47 us (3%)
    pallas_call x1, Pallas kernels, per_device(): pl.pallas_call(finish, out_shape=(jax.ShapeDtypeStruct((columns, width, l...  81.7 us
    pallas_call x1, Pallas kernels, per_device(): pl.pallas_call(functools.partial(kernel, strips), out_shape=(pltpu.VMEM((...  18.2 us
    unnamed x8, local copies, waits for them, and re-layouts  3.47 us

profile of v4, /device:TPU:0, one launch (start us, length us, event | category | flops | bytes accessed | tf_op | source)
XLA Modules:
  0.0 104.0 jit_solution(3272025101207383090)
XLA Ops:
  0.6 18.2 %shard_map.122 = (bf16[8,256,640]{2,1,0:T(8,128)(2,1)S(1)}, bf16[4,128,256]{2,1,0:T(8,128)(2,1)S(1)}, bf16[256,128]{1,0:T(8,128)(2,1)S(1)}, bf16[256,256]{1,0:T(8,128)(2,1)S(1)}, s32[16]{0:T(128)}) custom-call(s32[3,16]{1,0:T(4,128)} %bitcast.5, s32[16]{0:T(128)} %mask_hbm.1, bf16[8,48,640]{2,1,0:T(8,128)(2,1)} %atm_hbm.1, bf16[95,16,128]{2,1,0:T(8,128)(2,1)} %bitcast.3, ...), custom_call_target="tpu_custom_call" | custom-call | flops 1509949440 | bytes 8388608 | tf_op jit(solution)/shard_map/pallas_call | solution.py:319
  18.8 0.0 copy-start
  18.9 1.5 %copy-done = bf16[8,256,640]{2,1,0:T(8,128)(2,1)} copy-done((bf16[8,256,640]{2,1,0:T(8,128)(2,1)}, bf16[8,256,640]{2,1,0:T(8,128)(2,1)S(1)}, u32[]{:S(2)}) %copy-start) | copy-done | bytes 2621464
  20.3 0.0 copy-start.1
  20.3 0.7 copy-done.1
  21.0 0.0 copy-start.2
  21.0 0.7 copy-done.2
  21.7 0.0 copy-start.3
  21.7 0.6 copy-done.3
  22.3 81.7 %shard_map.123 = (bf16[8,256,640]{2,1,0:T(8,128)(2,1)}, bf16[16,256,128]{2,1,0:T(8,128)(2,1)}) custom-call(s32[16]{0:T(128)} %get-tuple-element.7.from_hbm, bf16[8,256,640]{2,1,0:T(8,128)(2,1)} %copy-done, bf16[4,128,256]{2,1,0:T(8,128)(2,1)} %copy-done.1, bf16[256,128]{1,0:T(8,128)(2,1)} %copy-done.3, bf16[256,256]{1,0:T(8,128)(2,1)} %copy-done.2), custom_call_target="tpu_custom_call" | custom-call | flops 201326592 | bytes 8388608 | tf_op jit(solution)/shard_map/pallas_call | solution.py:371
Async XLA Ops:
  18.8 1.5 %copy-start = (bf16[8,256,640]{2,1,0:T(8,128)(2,1)}, bf16[8,256,640]{2,1,0:T(8,128)(2,1)S(1)}, u32[]{:S(2)}) copy-start(bf16[8,256,640]{2,1,0:T(8,128)(2,1)S(1)} %get-tuple-element.8.hid_in) | copy-start | bytes 7864324
  20.3 0.7 copy-start.1
  21.0 0.7 copy-start.2
  21.7 0.6 copy-start.3

commit v5 on v4

--- a/solution.py
+++ b/solution.py
@@ -56,8 +56,8 @@
 def kernel(
     strips,
     pair_hbm, mask_hbm, atm_hbm, ocean_hbm, lift_hbm, conv_hbm, flux_hbm, ow_hbm, cw_hbm, mix_hbm, regrid_hbm,
-    hid_out, packed_out, wocean_out, mixt_out, from_hbm,
-    pair_ref, mask_ref, from_ref, lift_ref, flux_ref, ow_ref, cw_ref, mix_ref, xin, conv_v, ocean_v, regrid_v, col, folded_f, wt, lt, ocean_f, ustate, mine, sides, mirror, partial,
+    hid_out, packed_out, wocean_out, mixt_out, from_out,
+    pair_ref, mask_ref, lift_ref, flux_ref, ow_ref, cw_ref, mix_ref, xin, conv_v, ocean_v, regrid_v, col, folded_f, wt, lt, ocean_f, ustate, mine, sides, mirror, partial,
     load_sem, regrid_sem, halo_send, halo_recv, flux_send, flux_recv, mir_sem,
 ):
     columns, channels, lat = atm_hbm.shape
@@ -209,12 +209,13 @@
 
     slots = water_slots(mask_ref, tiles)
     ahead = jnp.int32(0)
+    lane = lax.broadcasted_iota(jnp.int32, from_out.shape, 1)
+    origin = jnp.full(from_out.shape, MAXACT, jnp.int32)
     for t in range(tiles):
         slot = ahead if t < tiles - FOLDB else jnp.int32(MAXACT - tiles + t)
-        from_ref[t] = jnp.where(mask_ref[t] == 1, slot, MAXACT)
+        origin = jnp.where(lane == t, jnp.where(mask_ref[t] == 1, slot, MAXACT), origin)
         ahead = ahead + mask_ref[t]
-    give_from = pltpu.make_async_copy(from_ref, from_hbm, load_sem.at[10])
-    give_from.start()
+    from_out[...] = origin
     for k, t in enumerate(slots):
         packed_out[k // 2, :, (k % 2) * LANES : (k % 2 + 1) * LANES] = ustate[t]
 
@@ -251,7 +252,6 @@
 
     lax.fori_loop(0, chunks, arrive, 0)
     to_fold.wait()
-    give_from.wait()
 
     for k, t in enumerate(slots):
         blocks, got = (0, 2), [sides[p // 2, pair_ref[p, t]] for p in (0, 2)]
@@ -264,13 +264,11 @@
 
 
 def finish(
-    from_hbm, hid_in, packed, wocean, mixt,
+    from_in, hid_in, packed, wocean, mixt,
     hid_hbm, oce_hbm,
-    from_ref, oce, from_sem, hid_sem, oce_sem,
+    oce, hid_sem, oce_sem,
 ):
     tiles, width = oce_hbm.shape[:2]
-    get_from = pltpu.make_async_copy(from_hbm, from_ref, from_sem)
-    get_from.start()
     keep = pltpu.make_async_copy(hid_in, hid_hbm, hid_sem)
     keep.start()
     oce[MAXACT] = jnp.zeros((width, LANES), BF16)
@@ -281,8 +279,8 @@
         oce[k] = result[:, :LANES]
         oce[k + 1] = result[:, LANES:]
 
-    get_from.wait()
-    copies = [pltpu.make_async_copy(oce.at[from_ref[t]], oce_hbm.at[t], oce_sem.at[t]) for t in range(tiles)]
+    origin = from_in[...]
+    copies = [pltpu.make_async_copy(oce.at[origin[0, t]], oce_hbm.at[t], oce_sem.at[t]) for t in range(tiles)]
     for copy in copies:
         copy.start()
     for copy in copies:
@@ -323,13 +321,12 @@
             pltpu.VMEM((MAXACT // 2, LANES, 2 * cells), BF16),
             pltpu.VMEM((width, LANES), BF16),
             pltpu.VMEM((width, width), BF16),
-            jax.ShapeDtypeStruct((tiles,), jnp.int32),
+            pltpu.VMEM((8, LANES), jnp.int32),
         ),
         in_specs=[hbm] * 11,
-        out_specs=(vmem,) * 4 + (anywhere,),
+        out_specs=(vmem,) * 5,
         scratch_shapes=[
             pltpu.SMEM(pair_tile.shape[::-1], jnp.int32),
-            pltpu.SMEM(ocean_mask.shape, jnp.int32),
             pltpu.SMEM(ocean_mask.shape, jnp.int32),
             pltpu.VMEM(lift_weight.shape, BF16),
             pltpu.VMEM(flux_weight.shape[::-1], BF16),
@@ -350,7 +347,7 @@
             pltpu.VMEM((2, lat // TLAT, fl, LANES), BF16),
             pltpu.VMEM((fl, LANES), BF16),
             pltpu.VMEM((MAXACT, 2 * fl, LANES), F32),
-            dma((11,)),
+            dma((10,)),
             dma((2,)),
             dma((2,)),
             dma((2,)),
@@ -359,7 +356,7 @@
             dma((2,)),
         ],
         compiler_params=pltpu.CompilerParams(
-            collective_id=0, has_side_effects=True, vmem_limit_bytes=61 * 1024 * 1024
+            collective_id=0, has_side_effects=True, vmem_limit_bytes=62432 * 1024
         ),
         cost_estimate=pl.CostEstimate(
             flops=24 * columns * lat * width * channels, bytes_accessed=8 * 1024 * 1024, transcendentals=1024 * 1024
@@ -374,16 +371,14 @@
             jax.ShapeDtypeStruct((columns, width, lat), BF16),
             jax.ShapeDtypeStruct((tiles, width, cells), BF16),
         ),
-        in_specs=[anywhere, anywhere, vmem, vmem, vmem],
+        in_specs=[vmem, anywhere, vmem, vmem, vmem],
         out_specs=(anywhere, anywhere),
         scratch_shapes=[
-            pltpu.SMEM((tiles,), jnp.int32),
             pltpu.VMEM((MAXACT + 1, width, cells), BF16),
-            dma,
             dma,
             dma((tiles,)),
         ],
-        compiler_params=pltpu.CompilerParams(vmem_limit_bytes=61 * 1024 * 1024),
+        compiler_params=pltpu.CompilerParams(vmem_limit_bytes=50 * 1024 * 1024),
         cost_estimate=pl.CostEstimate(
             flops=2 * MAXACT * cells * width * (width + 128), bytes_accessed=8 * 1024 * 1024, transcendentals=1024 * 1024
         ),

time: 104 us -> 21.4 us (0.21)
  Pallas kernels: 99.9 us -> 20.6 us
  local copies, waits for them, and re-layouts: 3.47 us -> 0 us
    pallas_call x1, Pallas kernels: 81.7 us -> 2.43 us  [per_device(): pl.pallas_call(finish, out_shape=(jax.ShapeDtypeStruct((columns, width, l...]
    unnamed x8 -> x0, local copies, waits for them, and re-layouts: 3.47 us -> none
where the time goes in v5:
time: 21.4 us; the launch traced here: 21.2 us
  Pallas kernels  20.6 us (96%)
  between operations  0.64 us (3%)
    pallas_call x1, Pallas kernels, per_device(): pl.pallas_call(functools.partial(kernel, strips), out_shape=(pltpu.VMEM((...  18.2 us
    pallas_call x1, Pallas kernels, per_device(): pl.pallas_call(finish, out_shape=(jax.ShapeDtypeStruct((columns, width, l...  2.43 us

profile of v5, /device:TPU:0, one launch (start us, length us, event | category | flops | bytes accessed | tf_op | source)
XLA Modules:
  0.0 21.2 jit_solution(13940838764012428784)
XLA Ops:
  0.6 18.2 %shard_map.122 = (bf16[8,256,640]{2,1,0:T(8,128)(2,1)S(1)}, bf16[4,128,256]{2,1,0:T(8,128)(2,1)S(1)}, bf16[256,128]{1,0:T(8,128)(2,1)S(1)}, bf16[256,256]{1,0:T(8,128)(2,1)S(1)}, s32[8,128]{1,0:T(8,128)S(1)}) custom-call(s32[3,16]{1,0:T(4,128)} %bitcast.5, s32[16]{0:T(128)} %mask_hbm.1, bf16[8,48,640]{2,1,0:T(8,128)(2,1)} %atm_hbm.1, ...), custom_call_target="tpu_custom_call" | custom-call | flops 1509949440 | bytes 8388608 | tf_op jit(solution)/shard_map/pallas_call | solution.py:317
  18.8 2.4 %shard_map.123 = (bf16[8,256,640]{2,1,0:T(8,128)(2,1)}, bf16[16,256,128]{2,1,0:T(8,128)(2,1)}) custom-call(s32[8,128]{1,0:T(8,128)S(1)} %get-tuple-element.7.from_in, bf16[8,256,640]{2,1,0:T(8,128)(2,1)S(1)} %get-tuple-element.8.hid_in, bf16[4,128,256]{2,1,0:T(8,128)(2,1)S(1)} %get-tuple-element.9.packed, bf16[256,128]{1,0:T(8,128)(2,1)S(1)} %get-tuple-element.10.wocean, ...), custom_call_target="tpu_custom_call" | custom-call | flops 201326592 | bytes 8388608 | tf_op jit(solution)/shard_map/pallas_call | solution.py:368

commit v6 on v5

--- a/solution.py
+++ b/solution.py
@@ -58,7 +58,7 @@
     pair_hbm, mask_hbm, atm_hbm, ocean_hbm, lift_hbm, conv_hbm, flux_hbm, ow_hbm, cw_hbm, mix_hbm, regrid_hbm,
     hid_out, packed_out, wocean_out, mixt_out, from_out,
     pair_ref, mask_ref, lift_ref, flux_ref, ow_ref, cw_ref, mix_ref, xin, conv_v, ocean_v, regrid_v, col, folded_f, wt, lt, ocean_f, ustate, mine, sides, mirror, partial,
-    load_sem, regrid_sem, halo_send, halo_recv, flux_send, flux_recv, mir_sem,
+    load_sem, conv_sem, regrid_sem, halo_send, halo_recv, flux_send, flux_recv, mir_sem,
 ):
     columns, channels, lat = atm_hbm.shape
     width = lift_ref.shape[1]
@@ -84,7 +84,9 @@
         pl.semaphore_signal(barrier, inc=1, device_id={"lon": other}, device_id_type=MESH)
 
     load_atm = pltpu.make_async_copy(atm_hbm, xin.at[pl.ds(1, columns)], load_sem.at[0])
-    load_conv = pltpu.make_async_copy(conv_hbm, conv_v, load_sem.at[1])
+    load_conv = [
+        pltpu.make_async_copy(conv_hbm.at[k // 3, k % 3], conv_v.at[k // 3, k % 3], conv_sem.at[k]) for k in range(9)
+    ]
     load_ocean = pltpu.make_async_copy(ocean_hbm, ocean_v, load_sem.at[2])
     load_main = pltpu.make_async_copy(
         regrid_hbm.at[:, pl.ds(0, 3)], regrid_v.at[:, pl.ds(0, 3)], regrid_sem.at[0]
@@ -106,7 +108,8 @@
     ]
     smalls[0].start()
     load_atm.start()
-    load_conv.start()
+    for load in load_conv:
+        load.start()
     for small in smalls[1:]:
         small.start()
 
@@ -135,7 +138,6 @@
                 col[c, at : at + channels, :] = piece[:, c * LANES : (c + 1) * LANES]
 
     load_atm.wait()
-    load_conv.wait()
     load_ocean.start()
     for load in load_ows:
         load.start()
@@ -144,6 +146,9 @@
     for small in smalls[1:]:
         small.wait()
     for k in range(9):
+        if k % 3 == 0:
+            for load in load_conv[k : k + 3]:
+                load.wait()
         folded_f[k * channels : (k + 1) * channels, :] = dot(lift_ref[...], conv_v[k // 3, k % 3])
         if k < columns:
             spread(k + 1)
@@ -194,8 +199,8 @@
     flux = {}
     bands = list(reversed(range(chunks)))
     sweep([(c, x) for c in bands for x in range(2, columns - 2, 2)])
-    halo_r.wait()
-    halo_l.wait()
+    halo_r.wait_recv()
+    halo_l.wait_recv()
     spread(0)
     spread(columns + 1)
 
@@ -246,12 +251,12 @@
         partial[k] = weigh(t, (1,), [mine[pair_ref[1, t]]])
 
     def arrive(c, carry):
-        flux_copy(c, right, 0).wait()
-        flux_copy(c, left, 1).wait()
+        flux_copy(c, right, 0).wait_recv()
+        flux_copy(c, left, 1).wait_recv()
         return carry
 
     lax.fori_loop(0, chunks, arrive, 0)
-    to_fold.wait()
+    to_fold.wait_recv()
 
     for k, t in enumerate(slots):
         blocks, got = (0, 2), [sides[p // 2, pair_ref[p, t]] for p in (0, 2)]
@@ -262,6 +267,16 @@
             sums[:fl] / sums[fl : fl + 1]
         ).astype(BF16)
 
+    def leave(c, carry):
+        flux_copy(c, right, 0).wait_send()
+        flux_copy(c, left, 1).wait_send()
+        return carry
+
+    lax.fori_loop(0, chunks, leave, 0)
+    to_fold.wait_send()
+    for halo in (halo_r, halo_l):
+        halo.wait_send()
+
 
 def finish(
     from_in, hid_in, packed, wocean, mixt,
@@ -269,8 +284,9 @@
     oce, hid_sem, oce_sem,
 ):
     tiles, width = oce_hbm.shape[:2]
-    keep = pltpu.make_async_copy(hid_in, hid_hbm, hid_sem)
-    keep.start()
+    keeps = [pltpu.make_async_copy(hid_in.at[x], hid_hbm.at[x], hid_sem.at[x]) for x in range(hid_in.shape[0])]
+    for keep in keeps:
+        keep.start()
     oce[MAXACT] = jnp.zeros((width, LANES), BF16)
     for k in range(0, MAXACT, 2):
         base = dot(wocean[...], packed[k // 2]).astype(BF16)
@@ -285,7 +301,8 @@
         copy.start()
     for copy in copies:
         copy.wait()
-    keep.wait()
+    for keep in keeps:
+        keep.wait()
 
 
 def per_device(
@@ -348,6 +365,7 @@
             pltpu.VMEM((fl, LANES), BF16),
             pltpu.VMEM((MAXACT, 2 * fl, LANES), F32),
             dma((10,)),
+            dma((9,)),
             dma((2,)),
             dma((2,)),
             dma((2,)),
@@ -375,7 +393,7 @@
         out_specs=(anywhere, anywhere),
         scratch_shapes=[
             pltpu.VMEM((MAXACT + 1, width, cells), BF16),
-            dma,
+            dma((columns,)),
             dma((tiles,)),
         ],
         compiler_params=pltpu.CompilerParams(vmem_limit_bytes=50 * 1024 * 1024),

time: 21.4 us -> 21.6 us (level)
  no operation moved by 1% of the time
where the time goes in v6:
time: 21.6 us; the launch traced here: 21.4 us
  Pallas kernels  20.8 us (96%)
  between operations  0.64 us (3%)
    pallas_call x1, Pallas kernels, per_device(): pl.pallas_call(functools.partial(kernel, strips), out_shape=(pltpu.VMEM((...  18.3 us
    pallas_call x1, Pallas kernels, per_device(): pl.pallas_call(finish, out_shape=(jax.ShapeDtypeStruct((columns, width, l...  2.5 us

profile of v6, /device:TPU:0, one launch (start us, length us, event | category | flops | bytes accessed | tf_op | source)
XLA Modules:
  0.0 21.4 jit_solution(7205953207145868354)
XLA Ops:
  0.6 18.3 %shard_map.122 = (bf16[8,256,640]{2,1,0:T(8,128)(2,1)S(1)}, bf16[4,128,256]{2,1,0:T(8,128)(2,1)S(1)}, bf16[256,128]{1,0:T(8,128)(2,1)S(1)}, bf16[256,256]{1,0:T(8,128)(2,1)S(1)}, s32[8,128]{1,0:T(8,128)S(1)}) custom-call(s32[3,16]{1,0:T(4,128)} %bitcast.5, s32[16]{0:T(128)} %mask_hbm.1, bf16[8,48,640]{2,1,0:T(8,128)(2,1)} %atm_hbm.1, ...), custom_call_target="tpu_custom_call" | custom-call | flops 1509949440 | bytes 8388608 | tf_op jit(solution)/shard_map/pallas_call | solution.py:334
  18.9 2.5 %shard_map.123 = (bf16[8,256,640]{2,1,0:T(8,128)(2,1)}, bf16[16,256,128]{2,1,0:T(8,128)(2,1)}) custom-call(s32[8,128]{1,0:T(8,128)S(1)} %get-tuple-element.7.from_in, bf16[8,256,640]{2,1,0:T(8,128)(2,1)S(1)} %get-tuple-element.8.hid_in, bf16[4,128,256]{2,1,0:T(8,128)(2,1)S(1)} %get-tuple-element.9.packed, bf16[256,128]{1,0:T(8,128)(2,1)S(1)} %get-tuple-element.10.wocean, ...), custom_call_target="tpu_custom_call" | custom-call | flops 201326592 | bytes 8388608 | tf_op jit(solution)/shard_map/pallas_call | solution.py:386
